TPU v7x, 128 devices: a whole 4x4x4 slice. The times are simulated.
128 devices in a mesh: req: 4 (over y), tile: 32 (over x, z, core).
Axes of the slice: x: 4, y: 4, z: 4, core: 2. Of those that a mesh axis runs over, the one named last changes fastest.
Arguments:
- latent: bfloat16 [16, 4, 64, 32, 16], P('req', None, 'tile'), may hold values from -6 to 6
- destination: int32 [16, 1], replicated, may hold values from 0 to 3; in each aligned block of 4 rows (0 to 3, 4 to 7, ...) at most 2 rows name the same one
- valid_frames: int32 [16], replicated, may hold values from 1 to 4
- cache_slot: int32 [16], replicated, may hold values from 0 to 15, each once
- latent_cache: bfloat16 [64, 2, 64, 32, 16], P('req', None, 'tile'), may hold values from -6 to 6
- feature_cache: bfloat16 [64, 2, 64, 32, 384], P('req', None, 'tile'), may hold values from -6 to 6
- in_weight: bfloat16 [3, 3, 3, 16, 384], replicated, may hold values from -0.3125 to 0.3125
- in_bias: float32 [384], replicated, may hold values from -4 to 4
- norm_gain: float32 [384], replicated, may hold values from 0.1 to 1.9
- time_weight: bfloat16 [3, 384, 768], replicated, may hold values from -0.1875 to 0.1875
- time_bias: float32 [768], replicated, may hold values from -3 to 3
- out_weight: bfloat16 [3, 3, 384, 192], replicated, may hold values from -0.109375 to 0.109375
- out_bias: float32 [192], replicated, may hold values from -3 to 3
Outputs:
- decoded: bfloat16 [32, 8, 128, 64, 192], P('req', None, 'tile')
Inputs may be any that keep to these rules, and one draw needn't show every extreme that they name: `destination`: request r starts on index r // 4 of req. Among the 4 requests of one index no group is named more than 2 times, and in some such block one group is named exactly 2 times. `cache_slot`: each value once.
All inputs are finite; a program needn't handle non-finite values.
Results may differ from a plain program's by a relative error of at most 0.0051.
Values may be sent and summed in bfloat16 or wider, within the bound.
A program may use at most 320 MiB of HBM per device.

v0:
```python
import jax
import jax.numpy as jnp
from jax import lax
from jax.sharding import PartitionSpec as P

LATENT_CHANNELS = 16
MIDDLE_CHANNELS = 384
OUTPUT_CHANNELS = 192
FRAMES = 4
CAPACITY = 2


EPSILON = 1e-06


def with_halo(shard, sides, width):
    for axis, dim in sides:
        count, length = (lax.axis_size(axis), shard.shape[dim])
        up = [(i, (i + 1) % count) for i in range(count - 1)]
        down = [(j, i) for i, j in up]
        last = lax.slice_in_dim(shard, length - width, length, axis=dim)
        first = lax.slice_in_dim(shard, 0, width, axis=dim)
        before = lax.ppermute(last, axis, up)
        after = lax.ppermute(first, axis, down)
        shard = jnp.concatenate([before, shard, after], axis=dim)
    return shard


def rank_within(flat_target, per_source):
    positions = jnp.arange(flat_target.shape[0])
    source = positions // per_source
    earlier = (
        (source[:, None] == source[None, :])
        & (flat_target[:, None] == flat_target[None, :])
        & (positions[None, :] < positions[:, None])
    )
    return (source, jnp.sum(earlier.astype(jnp.int32), axis=1))


def patch_stack(padded, row_count, column_count):
    pieces = []
    for time_step in range(3):
        for row_step in range(3):
            for column_step in range(3):
                pieces.append(
                    padded[
                        ...,
                        time_step : time_step + FRAMES,
                        row_step : row_step + row_count,
                        column_step : column_step + column_count,
                        :,
                    ]
                )
    return jnp.concatenate(pieces, axis=-1)


def normed_silu(inner_sum, norm_gain):
    norm_scale = lax.rsqrt(jnp.mean(inner_sum * inner_sum, axis=-1, keepdims=True) + EPSILON)
    return jax.nn.silu(inner_sum * norm_scale * norm_gain)


def temporal(sequence, time_weight, time_bias):
    running = time_bias
    for time_step in range(3):
        running = running + jnp.dot(
            sequence[..., time_step : time_step + FRAMES, :, :, :],
            time_weight[time_step],
            preferred_element_type=jnp.float32,
        )
    return running


def spatial_conv(padded, out_weight, row_count, column_count):
    running = jnp.zeros(
        padded.shape[:-3] + (row_count, column_count, out_weight.shape[-1]), jnp.float32
    )
    for row_step in range(3):
        for column_step in range(3):
            running = running + jnp.dot(
                padded[
                    ...,
                    row_step : row_step + row_count,
                    column_step : column_step + column_count,
                    :,
                ],
                out_weight[row_step, column_step],
                preferred_element_type=jnp.float32,
            )
    return running


def split_halves(doubled):
    halves = jnp.stack([doubled[..., :MIDDLE_CHANNELS], doubled[..., MIDDLE_CHANNELS:]], axis=2)
    return halves.reshape((-1,) + halves.shape[3:])


def enlarge(frames):
    return jnp.repeat(jnp.repeat(frames, 2, axis=1), 2, axis=2)


def per_device(
    latent,
    destination,
    valid_frames,
    cache_slot,
    latent_cache,
    feature_cache,
    in_weight,
    in_bias,
    norm_gain,
    time_weight,
    time_bias,
    out_weight,
    out_bias,
):
    group_index = lax.axis_index("req")
    group_count = lax.axis_size("req")
    local_count = latent.shape[0]
    row_count = latent.shape[2]
    frame_width = latent.shape[3]
    slot_count = group_count * CAPACITY
    flat_target = destination[:, 0]
    source, order_rank = rank_within(flat_target, local_count)
    position = source * CAPACITY + order_rank
    mine_start = group_index * local_count
    send_slot = lax.dynamic_slice_in_dim(
        flat_target * CAPACITY + order_rank, mine_start, local_count
    )
    picker = (jnp.arange(slot_count)[:, None] == send_slot[None, :]).astype(jnp.bfloat16)
    packed = latent.reshape(local_count, FRAMES * row_count * frame_width * LATENT_CHANNELS)
    outgoing = jnp.dot(picker, packed, preferred_element_type=jnp.float32).astype(jnp.bfloat16)
    outgoing = outgoing.reshape(slot_count, FRAMES, row_count, frame_width * LATENT_CHANNELS)
    arrived = lax.all_to_all(outgoing, "req", split_axis=0, concat_axis=0, tiled=True)
    landing = (flat_target == group_index)[None, :] & (
        position[None, :] == jnp.arange(slot_count)[:, None]
    )
    slot_frames = jnp.sum(jnp.where(landing, valid_frames[None, :], 0), axis=1)
    slot_row = jnp.sum(jnp.where(landing, cache_slot[None, :], 0), axis=1)
    earlier_latent = latent_cache[slot_row].reshape(
        slot_count, 2, row_count, frame_width * LATENT_CHANNELS
    )
    kept_frames = jnp.arange(FRAMES)[None, :] < slot_frames[:, None]
    masked = jnp.where(kept_frames[:, :, None, None], arrived, jnp.zeros_like(arrived))
    sequence = jnp.concatenate([earlier_latent, masked], axis=1)
    rimmed = with_halo(sequence, (("tile", 2),), 1)
    rimmed = rimmed.reshape(slot_count, FRAMES + 2, row_count + 2, frame_width, LATENT_CHANNELS)
    padded = jnp.pad(rimmed, ((0, 0), (0, 0), (0, 0), (1, 1), (0, 0)))
    stacked = patch_stack(padded, row_count, frame_width)
    flat_in = in_weight.reshape(27 * LATENT_CHANNELS, MIDDLE_CHANNELS)
    inner_sum = jnp.dot(stacked, flat_in, preferred_element_type=jnp.float32) + in_bias
    active = normed_silu(inner_sum, norm_gain).astype(jnp.bfloat16)
    middle_sequence = jnp.concatenate([feature_cache[slot_row], active], axis=1)
    frame_total = slot_count * 2 * FRAMES
    doubled = temporal(middle_sequence, time_weight, time_bias).astype(jnp.bfloat16)
    plain_frames = enlarge(split_halves(doubled)).reshape(
        frame_total, 2 * row_count, 2 * frame_width * MIDDLE_CHANNELS
    )
    upsampled = with_halo(plain_frames, (("tile", 1),), 1)
    upsampled = upsampled.reshape(frame_total, 2 * row_count + 2, 2 * frame_width, MIDDLE_CHANNELS)
    padded_up = jnp.pad(upsampled, ((0, 0), (0, 0), (1, 1), (0, 0)))
    result = spatial_conv(padded_up, out_weight, 2 * row_count, 2 * frame_width) + out_bias
    result = result.reshape(slot_count, 2 * FRAMES, 2 * row_count, 2 * frame_width, OUTPUT_CHANNELS)
    shown_frames = (jnp.arange(2 * FRAMES) // 2)[None, :] < slot_frames[:, None]
    return jnp.where(shown_frames[:, :, None, None, None], result, 0.0).astype(jnp.bfloat16)


def solution(mesh):
    placed = (
        P("req", None, "tile", None, None),
        P(),
        P(),
        P(),
        P("req", None, "tile", None, None),
        P("req", None, "tile", None, None),
        P(),
        P(),
        P(),
        P(),
        P(),
        P(),
        P(),
    )
    return jax.shard_map(
        per_device,
        mesh=mesh,
        in_specs=placed,
        out_specs=P("req", None, "tile", None, None),
        check_vma=False,
    )
```

profile of v0, /device:TPU:6, one launch (start us, length us, event | category | flops | bytes accessed | tf_op | source)
XLA Modules:
  0.0 357.5 jit_solution(11607241674342159082)
XLA Ops:
  3.9 4.5 %all-to-all-start = ((bf16[8,4,2,512]{3,2,1,0:T(2,128)(2,1)}), bf16[8,4,2,512]{3,2,1,0:T(2,128)(2,1)S(1)}, u32[]{:S(2)}, u32[]{:S(2)}) async-start(bf16[8,4,2,512]{3,2,1,0:T(2,128)(2,1)} %copy.49), calls=%async_computation | async-start | bytes 131072 | tf_op jit(solution)/shard_map/all_to_all | solution.py:133
  11.9 2.1 all-to-all-done
  14.3 1.9 collective-permute-start
  16.3 5.8 %collective-permute-start.1 = (bf16[8,6,1,512]{3,2,1,0:T(2,128)(2,1)S(1)}, bf16[8,6,1,512]{3,2,1,0:T(2,128)(2,1)S(1)}, u32[]{:S(2)}, u32[]{:S(2)}) collective-permute-start(bf16[8,6,1,512]{3,2,1,0:T(2,128)(2,1)S(1)} %get-tuple-element.39), channel_id=1, source_target_pairs={{1,0},{2,1},{3,2},{4,3},{5,4},{6,5},{7,6},{8,7},{9,8},{10,9},{11,1... | collective-permute-start | bytes 147464 | tf_op jit(solution)/shard_map/ppermute | solution.py:24
  25.7 2.4 fusion.64
  28.1 5.6 %pad_slice_fusion = (bf16[8,4,2,32,16]{4,3,2,1,0:T(8,128)(2,1)}, bf16[8,4,2,32,16]{4,3,2,1,0:T(8,128)(2,1)}, bf16[8,4,2,32,16]{4,3,2,1,0:T(8,128)(2,1)}, bf16[8,...) fusion(bf16[8,6,4,32,16]{4,3,2,1,0:T(8,128)(2,1)S(1)} %reshape.194), kind=kLoop, calls=%fused_computation.42 | loop fusion | bytes 3866624 | tf_op jit(solution)/shard_map/slice | solution.py:46
  33.7 13.1 %concatenate.30 = bf16[8,4,2,32,432]{4,3,2,1,0:T(8,128)(2,1)} concatenate(bf16[8,4,2,32,16]{4,3,2,1,0:T(8,128)(2,1)} %get-tuple-element.37, bf16[8,4,2,32,16]{4,3,2,1,0:T(8,128)(2,1)} %get-tuple-element.36, bf16[8,4,2,32,16]{4,3,2,1,0:T(8,128)(2,1)} %get-tuple-element.12, bf16[8,4,2,32,16]{4,3,2,1,0:T(8,128)(2,1)} %get-tuple-element.13, ...), dimensions={4} | concatenate | bytes 3538944 | tf_op jit(solution)/shard_map/concatenate | solution.py:54
  46.8 3.1 multiply_reduce_fusion
  50.9 1.8 fusion.28
  52.8 1.8 fusion.29
  54.6 2.1 add_convert_fusion
  58.8 12.7 %broadcast_in_dim.78 = bf16[64,4,32,2,384]{4,3,2,1,0:T(2,128)(2,1)} broadcast(bf16[64,4,32,384]{3,2,1,0:T(8,128)(2,1)S(1)} %bitcast.127), dimensions={0,1,2,4} | broadcast | bytes 18874368 | tf_op jit(solution)/shard_map/broadcast_in_dim | solution.py:98
  71.5 28.1 %reshape.193 = bf16[64,4,24576]{2,1,0:T(4,128)(2,1)} reshape(bf16[64,4,32,2,384]{4,3,2,1,0:T(2,128)(2,1)} %broadcast_in_dim.78) | data formatting | bytes 25165824 | tf_op jit(solution)/shard_map/reshape;reshape | solution.py:155
  99.6 15.3 %fusion.63 = (bf16[64,1,24576]{2,1,0:T(2,128)(2,1)S(1)}, bf16[64,1,24576]{2,1,0:T(2,128)(2,1)S(1)}) fusion(bf16[64,4,24576]{2,1,0:T(4,128)(2,1)} %reshape.193), kind=kLoop, calls=%fused_computation.119 | loop fusion | bytes 12582912 | tf_op jit(solution)/shard_map/slice | solution.py:21
  114.9 5.1 %copy.82 = bf16[64,1,24576]{2,0,1:T(8,128)(2,1)} copy(bf16[64,1,24576]{2,1,0:T(2,128)(2,1)S(1)} %get-tuple-element.8) | data formatting | bytes 6291456
  120.0 5.8 %collective-permute-start.3 = (bf16[64,1,24576]{2,0,1:T(8,128)(2,1)}, bf16[64,1,24576]{2,0,1:T(8,128)(2,1)}, u32[]{:S(2)}, u32[]{:S(2)}) collective-permute-start(bf16[64,1,24576]{2,0,1:T(8,128)(2,1)} %copy.82), channel_id=1, source_target_pairs={{1,0},{2,1},{3,2},{4,3},{5,4},{6,5},{7,6},{8,7},{9,8},{10,9},{11,1... | collective-permute-start | bytes 9437192 | tf_op jit(solution)/shard_map/ppermute | solution.py:24
  125.8 5.0 %copy.81 = bf16[64,1,24576]{2,0,1:T(8,128)(2,1)} copy(bf16[64,1,24576]{2,1,0:T(2,128)(2,1)S(1)} %get-tuple-element.7) | data formatting | bytes 6291456
  130.9 1.9 collective-permute-start.2
  133.5 26.4 %concatenate.33 = bf16[64,4,64,384]{3,2,1,0:T(8,128)(2,1)} reshape(bf16[64,4,32,2,384]{4,3,2,1,0:T(2,128)(2,1)} %broadcast_in_dim.78) | data formatting | bytes 25165824 | tf_op jit(solution)/shard_map/concatenate | solution.py:25
  159.9 15.0 %fusion.40 = f32[64,4,64,192]{3,2,1,0:T(8,128)} fusion(bf16[64,4,64,384]{3,2,1,0:T(8,128)(2,1)} %concatenate.33, bf16[3,3,384,192]{2,3,1,0:T(8,128)(2,1)S(1)} %copy-done.5), kind=kOutput, calls=%fused_computation.71 | convolution fusion | flops 2415919104 | bytes 25313280 | tf_op jit(solution)/shard_map/dot_general | solution.py:79
  174.9 2.7 copy.84
  177.6 4.7 %copy.83 = bf16[8,8,64,384]{3,2,1,0:T(8,128)(2,1)} copy(bf16[8,8,64,384]{3,1,2,0:T(8,128)(2,1)} %bitcast.78) | data formatting | bytes 6291456
  182.4 9.6 %fusion.6 = f32[64,4,64,192]{3,2,1,0:T(8,128)} fusion(bf16[64,4,64,384]{3,2,1,0:T(8,128)(2,1)S(1)} %copy-done.2, bf16[64,1,64,384]{3,2,1,0:T(8,128)(2,1)} %bitcast.130, bf16[3,3,384,192]{2,3,1,0:T(8,128)(2,1)S(1)} %copy-done.5), kind=kOutput, calls=%fused_computation.12 | convolution fusion | flops 2447376384 | bytes 28459008 | tf_op jit(solution)/shard_map/dot_general | solution.py:79
  192.0 8.2 %fusion.10 = f32[64,4,64,192]{3,2,1,0:T(8,128)} fusion(bf16[64,1,64,384]{3,2,1,0:T(8,128)(2,1)S(1)} %bitcast.128, bf16[64,4,64,384]{3,2,1,0:T(8,128)(2,1)S(1)} %copy-done.2, bf16[3,3,384,192]{2,3,1,0:T(8,128)(2,1)S(1)} %copy-done.5), kind=kOutput, calls=%fused_computation.16 | convolution fusion | flops 2447376384 | bytes 28459008 | tf_op jit(solution)/shard_map/dot_general | solution.py:79
  200.2 21.8 %fusion.5 = bf16[64,6,66,384]{3,2,1,0:T(8,128)(2,1)} fusion(bf16[64,1,64,384]{3,2,1,0:T(8,128)(2,1)S(1)} %bitcast.129, bf16[64,4,64,384]{3,2,1,0:T(8,128)(2,1)S(1)} %copy-done.2, bf16[64,1,64,384]{3,2,1,0:T(8,128)(2,1)S(1)} %bitcast.131), kind=kLoop, calls=%fused_computation.9 | loop fusion | flops 116785152 | bytes 38338560 | tf_op jit(solution)/shard_map/concatenate | solution.py:25
  222.1 14.9 %fusion.18 = f32[64,4,64,192]{3,2,1,0:T(8,128)} fusion(bf16[64,6,66,384]{3,2,1,0:T(8,128)(2,1)} %fusion.5, bf16[3,3,384,192]{2,3,1,0:T(8,128)(2,1)S(1)} %copy-done.5), kind=kOutput, calls=%fused_computation.22 | convolution fusion | flops 2415919104 | bytes 25313280 | tf_op jit(solution)/shard_map/dot_general | solution.py:79
  237.0 15.4 %fusion.20 = f32[64,4,64,192]{3,2,1,0:T(8,128)} fusion(bf16[64,6,66,384]{3,2,1,0:T(8,128)(2,1)} %fusion.5, bf16[3,3,384,192]{2,3,1,0:T(8,128)(2,1)S(1)} %copy-done.5), kind=kOutput, calls=%fused_computation.24 | convolution fusion | flops 2415919104 | bytes 25313280 | tf_op jit(solution)/shard_map/dot_general | solution.py:79
  252.3 15.1 %fusion.22 = f32[64,4,64,192]{3,2,1,0:T(8,128)} fusion(bf16[64,6,66,384]{3,2,1,0:T(8,128)(2,1)} %fusion.5, bf16[3,3,384,192]{2,3,1,0:T(8,128)(2,1)S(1)} %copy-done.5), kind=kOutput, calls=%fused_computation.26 | convolution fusion | flops 2415919104 | bytes 25313280 | tf_op jit(solution)/shard_map/dot_general | solution.py:79
  267.4 15.3 %fusion.24 = f32[64,4,64,192]{3,2,1,0:T(8,128)} fusion(bf16[64,6,66,384]{3,2,1,0:T(8,128)(2,1)} %fusion.5, bf16[3,3,384,192]{2,3,1,0:T(8,128)(2,1)S(1)} %copy-done.5), kind=kOutput, calls=%fused_computation.28 | convolution fusion | flops 2415919104 | bytes 25313280 | tf_op jit(solution)/shard_map/dot_general | solution.py:79
  282.7 14.9 %fusion.26 = f32[64,4,64,192]{3,2,1,0:T(8,128)} fusion(bf16[64,6,66,384]{3,2,1,0:T(8,128)(2,1)} %fusion.5, bf16[3,3,384,192]{2,3,1,0:T(8,128)(2,1)S(1)} %copy-done.5), kind=kOutput, calls=%fused_computation.30 | convolution fusion | flops 2415919104 | bytes 25313280 | tf_op jit(solution)/shard_map/dot_general | solution.py:79
  297.6 48.9 %add_add_fusion = bf16[64,4,64,192]{3,2,1,0:T(8,128)(2,1)} fusion(f32[64,4,64,192]{3,2,1,0:T(8,128)} %fusion.10, f32[64,4,64,192]{3,2,1,0:T(8,128)} %fusion.18, f32[64,4,64,192]{3,2,1,0:T(8,128)} %fusion.20, f32[64,4,64,192]{3,2,1,0:T(8,128)} %fusion.40, f32[64,4,64,192]{3,2,1,0:T(8,128)} %fusion.22, f32[64,4,64,192]{3,2,1,0:T(8,128)} %fusion.24, ...), kind=kOutput, calls=%fused_computation.11 | convolution fusion | flops 2447376384 | bytes 153240576 | tf_op jit(solution)/shard_map/dot_general | solution.py:79
  346.5 10.7 %select_convert_fusion = bf16[8,8,4,64,192]{4,3,2,1,0:T(8,128)(2,1)} fusion(bf16[8,8,4,64,192]{4,3,2,1,0:T(8,128)(2,1)} %bitcast.126, pred[8,8]{1,0:T(8,128)(4,1)S(1)} %copy-done.7), kind=kLoop, calls=%fused_computation.10 | loop fusion | flops 3145728 | bytes 12582976 | tf_op jit(solution)/shard_map/convert_element_type | solution.py:164
  (57 shorter events, 15.2 us)
Async XLA Ops:
  0.0 22.0 %copy-start = (bf16[16,2,2,32,384]{4,3,2,1,0:T(8,128)(2,1)S(1)}, bf16[16,2,2,32,384]{4,3,2,1,0:T(8,128)(2,1)}, u32[]{:S(2)}) copy-start(bf16[16,2,2,32,384]{4,3,2,1,0:T(8,128)(2,1)} %param.18) | copy-start | bytes 4718596
  3.9 10.1 %all-to-all-start = ((bf16[8,4,2,512]{3,2,1,0:T(2,128)(2,1)}), bf16[8,4,2,512]{3,2,1,0:T(2,128)(2,1)S(1)}, u32[]{:S(2)}, u32[]{:S(2)}) async-start(bf16[8,4,2,512]{3,2,1,0:T(2,128)(2,1)} %copy.49), calls=%async_computation | async-start | bytes 131072 | tf_op jit(solution)/shard_map/all_to_all | solution.py:133
  14.3 8.4 %collective-permute-start = (bf16[8,6,1,512]{3,2,1,0:T(2,128)(2,1)S(1)}, bf16[8,6,1,512]{3,2,1,0:T(2,128)(2,1)S(1)}, u32[]{:S(2)}, u32[]{:S(2)}) collective-permute-start(bf16[8,6,1,512]{3,2,1,0:T(2,128)(2,1)S(1)} %get-tuple-element.38), channel_id=1, source_target_pairs={{0,1},{1,2},{2,3},{3,4},{4,5},{5,6},{6,7},{7,8},{8,9},{9,10},{10,1... | collective-permute-start | bytes 147464 | tf_op jit(solution)/shard_map/ppermute | solution.py:23
  16.3 8.0 %collective-permute-start.1 = (bf16[8,6,1,512]{3,2,1,0:T(2,128)(2,1)S(1)}, bf16[8,6,1,512]{3,2,1,0:T(2,128)(2,1)S(1)}, u32[]{:S(2)}, u32[]{:S(2)}) collective-permute-start(bf16[8,6,1,512]{3,2,1,0:T(2,128)(2,1)S(1)} %get-tuple-element.39), channel_id=1, source_target_pairs={{1,0},{2,1},{3,2},{4,3},{5,4},{6,5},{7,6},{8,7},{9,8},{10,9},{11,1... | collective-permute-start | bytes 147464 | tf_op jit(solution)/shard_map/ppermute | solution.py:24
  33.7 13.1 %copy-start.8 = (f32[384]{0:T(512)S(1)}, f32[384]{0:T(512)}, u32[]{:S(2)}) copy-start(f32[384]{0:T(512)} %param.20) | copy-start | bytes 4612
  33.7 13.1 %copy-start.11 = (bf16[3,3,3,16,384]{4,3,2,1,0:T(8,128)(2,1)S(1)}, bf16[3,3,3,16,384]{4,3,2,1,0:T(8,128)(2,1)}, u32[]{:S(2)}) copy-start(bf16[3,3,3,16,384]{4,3,2,1,0:T(8,128)(2,1)} %param.19) | copy-start | bytes 995332
  46.8 3.2 copy-start.9
  46.8 4.1 %copy-start.4 = (bf16[3,384,768]{2,1,0:T(8,128)(2,1)S(1)}, bf16[3,384,768]{2,1,0:T(8,128)(2,1)}, u32[]{:S(2)}) copy-start(bf16[3,384,768]{2,1,0:T(8,128)(2,1)} %param.22) | copy-start | bytes 5308420
  52.7 1.8 copy-start.6
  120.0 54.9 %collective-permute-start.3 = (bf16[64,1,24576]{2,0,1:T(8,128)(2,1)}, bf16[64,1,24576]{2,0,1:T(8,128)(2,1)}, u32[]{:S(2)}, u32[]{:S(2)}) collective-permute-start(bf16[64,1,24576]{2,0,1:T(8,128)(2,1)} %copy.82), channel_id=1, source_target_pairs={{1,0},{2,1},{3,2},{4,3},{5,4},{6,5},{7,6},{8,7},{9,8},{10,9},{11,1... | collective-permute-start | bytes 9437192 | tf_op jit(solution)/shard_map/ppermute | solution.py:24
  130.9 46.7 %collective-permute-start.2 = (bf16[64,1,24576]{2,0,1:T(8,128)(2,1)}, bf16[64,1,24576]{2,0,1:T(8,128)(2,1)}, u32[]{:S(2)}, u32[]{:S(2)}) collective-permute-start(bf16[64,1,24576]{2,0,1:T(8,128)(2,1)} %copy.81), channel_id=1, source_target_pairs={{0,1},{1,2},{2,3},{3,4},{4,5},{5,6},{6,7},{7,8},{8,9},{9,10},{10,1... | collective-permute-start | bytes 9437192 | tf_op jit(solution)/shard_map/ppermute | solution.py:23
  133.5 26.4 %copy-start.5 = (bf16[3,3,384,192]{2,3,1,0:T(8,128)(2,1)S(1)}, bf16[3,3,384,192]{2,3,1,0:T(8,128)(2,1)}, u32[]{:S(2)}) copy-start(bf16[3,3,384,192]{2,3,1,0:T(8,128)(2,1)} %param.24) | copy-start | bytes 3981316
  174.9 7.5 %copy-start.2 = (bf16[64,4,64,384]{3,2,1,0:T(8,128)(2,1)S(1)}, bf16[64,4,64,384]{3,2,1,0:T(8,128)(2,1)}, u32[]{:S(2)}) copy-start(bf16[64,4,64,384]{3,2,1,0:T(8,128)(2,1)} %concatenate.33) | copy-start | bytes 37748740
  192.0 8.2 %copy-start.3 = (bf16[8,8,64,384]{3,2,1,0:T(8,128)(2,1)S(1)}, bf16[8,8,64,384]{3,2,1,0:T(8,128)(2,1)}, u32[]{:S(2)}) copy-start(bf16[8,8,64,384]{3,2,1,0:T(8,128)(2,1)} %copy.83) | copy-start | bytes 9437188
  282.7 14.9 %copy-start.10 = (f32[192]{0:T(256)S(1)}, f32[192]{0:T(256)}, u32[]{:S(2)}) copy-start(f32[192]{0:T(256)} %param.25) | copy-start | bytes 2308
  297.6 48.9 %copy-start.7 = (pred[8,8]{1,0:T(8,128)(4,1)S(1)}, pred[8,8]{1,0:T(8,128)(4,1)}, u32[]{:S(2)}) copy-start(pred[8,8]{1,0:T(8,128)(4,1)} %broadcast_compare_fusion) | copy-start | bytes 196
  346.5 10.8 %copy-start.1 = (bf16[16,2,2,32,384]{4,3,2,1,0:T(8,128)(2,1)S(1)}, bf16[16,2,2,32,384]{4,3,2,1,0:T(8,128)(2,1)}, u32[]{:S(2)}) copy-start(bf16[16,2,2,32,384]{4,3,2,1,0:T(8,128)(2,1)} %param.18) | copy-start | bytes 4718596
where the time goes:
time: 364 us; the launch traced here: 357 us
  matrix products  166 us (46%)
  local copies, waits for them, and re-layouts  129 us (35%)
  other arithmetic  38.4 us (11%)
  starting transfers between devices  19.9 us (5%)
    dot_general x9, matrix products, spatial_conv(): jnp.dot(padded[..., row_step:row_step + row_count, column_step:column_ste...  157 us
    another operation x1, local copies, waits for them, and re-layouts, per_device(): enlarge(split_halves(doubled))  28.1 us
    concatenate x1, local copies, waits for them, and re-layouts, with_halo(): shard = jnp.concatenate([before, shard, after], axis=dim)  26.4 us
    concatenate x2, other arithmetic, with_halo(): shard = jnp.concatenate([before, shard, after], axis=dim)  22.2 us
    unnamed x29, local copies, waits for them, and re-layouts  18.7 us
    slice x1, local copies, waits for them, and re-layouts, with_halo(): last = lax.slice_in_dim(shard, length - width, length, axis=dim)  15.3 us
    broadcast_in_dim x2, local copies, waits for them, and re-layouts, enlarge(): return jnp.repeat(jnp.repeat(frames, 2, axis=1), 2, axis=2)  13.4 us
    concatenate x1, local copies, waits for them, and re-layouts, patch_stack(): return jnp.concatenate(pieces, axis=-1)  13.1 us
  transfers between devices with their start and end apart: 5, of which 2 were waited for; matrix products, arithmetic and copies ran while one was open for 15% of the time, Pallas kernels for 0%

commit v1 on v0

v1 whole, which is shorter than its diff:
```python
import functools

import jax
import jax.numpy as jnp
from jax import lax
from jax.experimental import pallas as pl
from jax.experimental.pallas import tpu as pltpu
from jax.sharding import PartitionSpec as P

LATENT_CHANNELS = 16
MIDDLE_CHANNELS = 384
OUTPUT_CHANNELS = 192
FRAMES = 4
CAPACITY = 2
EPSILON = 1e-06

ROWS = 2
WIDTH = 32
WINDOW = (ROWS + 2) * WIDTH
PATCH = 9 * LATENT_CHANNELS
SEQ = FRAMES + 2
GROUP = 2

MESH = pl.DeviceIdType.MESH
BF16 = jnp.bfloat16
F32 = jnp.float32


def pick_two(dest_ref, start, target):
    seen = jnp.int32(0)
    first = jnp.int32(0)
    second = jnp.int32(0)
    for j in range(4):
        hit = dest_ref[start + j] == target
        first = jnp.where(hit & (seen == 0), j, first)
        second = jnp.where(hit & (seen == 1), j, second)
        seen = seen + hit.astype(jnp.int32)
    return first, second, seen


def lane_join(pieces):
    return jnp.concatenate([p.astype(F32) for p in pieces], axis=-1).astype(BF16)


def exchange_kernel(
    groups,
    tiles,
    dest_ref,
    cache_slot_ref,
    latent_ref,
    latent_cache_ref,
    feature_ref,
    out_weight_ref,
    latent_out,
    cache_out,
    feature_out,
    weight_out,
    latent_send,
    cache_send,
    feature_send,
    weight_scratch,
    latent_ssem,
    latent_rsem,
    cache_ssem,
    cache_rsem,
    feature_ssem,
    feature_rsem,
    weight_sem,
):
    group = lax.axis_index("req")
    tile = lax.axis_index("tile")

    def peer(offset, turn):
        return (lax.rem(group + turn, groups), lax.rem(tile + offset + tiles, tiles))

    barrier = pltpu.get_barrier_semaphore()
    for offset in (-1, 0, 1):
        for turn in range(4):
            if offset or turn:
                pl.semaphore_signal(barrier, inc=1, device_id=peer(offset, turn), device_id_type=MESH)

    for source in range(4):
        first, second, _ = pick_two(dest_ref, 4 * source, group)
        for k, local in ((0, first), (1, second)):
            row = cache_slot_ref[4 * source + local]
            slot = 2 * source + k
            for edge in range(2):
                for f in range(2):
                    feature_send[edge, slot, f] = feature_ref[row, f, edge]
            cache_send[slot] = lane_join(
                [latent_cache_ref[row, f, y] for f in range(2) for y in range(2)]
            )
    for turn in range(4):
        first, second, _ = pick_two(dest_ref, 4 * group, lax.rem(group + turn, groups))
        for k, local in ((0, first), (1, second)):
            for pair in range(2):
                latent_send[turn, k, pair] = lane_join(
                    [latent_ref[local, 2 * pair + f, y] for f in range(2) for y in range(2)]
                )

    pl.semaphore_wait(barrier, 11)
    copies = []
    for edge, offset, place in ((1, 1, 0), (0, -1, 1)):
        copies.append(
            pltpu.make_async_remote_copy(
                src_ref=feature_send.at[edge],
                dst_ref=feature_out.at[place],
                send_sem=feature_ssem.at[place],
                recv_sem=feature_rsem.at[place],
                device_id=peer(offset, 0),
                device_id_type=MESH,
            )
        )
    for offset in (1, -1, 0):
        place = 1 - offset
        for turn in range(4):
            if offset == 0 and turn == 0:
                copies.append(
                    pltpu.make_async_copy(
                        latent_send.at[0], latent_out.at[1, 0], latent_rsem.at[1, 0]
                    )
                )
            else:
                copies.append(
                    pltpu.make_async_remote_copy(
                        src_ref=latent_send.at[turn],
                        dst_ref=latent_out.at[place, turn],
                        send_sem=latent_ssem.at[place, turn],
                        recv_sem=latent_rsem.at[place, turn],
                        device_id=peer(offset, turn),
                        device_id_type=MESH,
                    )
                )
        if offset == 0:
            copies.append(pltpu.make_async_copy(cache_send, cache_out.at[1], cache_rsem.at[1]))
        else:
            copies.append(
                pltpu.make_async_remote_copy(
                    src_ref=cache_send,
                    dst_ref=cache_out.at[place],
                    send_sem=cache_ssem.at[place],
                    recv_sem=cache_rsem.at[place],
                    device_id=peer(offset, 0),
                    device_id_type=MESH,
                )
            )
    for copy in copies:
        copy.start()

    def combine(i, carry):
        at = pl.multiple_of(i * 16, 16)
        taps = [
            [out_weight_ref[b, c, pl.ds(at, 16), :].astype(F32) for c in range(3)] for b in range(3)
        ]
        rows = (
            (taps[0], [u + v for u, v in zip(taps[1], taps[2])]),
            ([u + v for u, v in zip(taps[0], taps[1])], taps[2]),
        )
        for py in range(2):
            for ty in range(2):
                line = rows[py][ty]
                columns = ((line[0], line[1] + line[2]), (line[0] + line[1], line[2]))
                for px in range(2):
                    for tx in range(2):
                        k = (2 * ty + tx) * MIDDLE_CHANNELS
                        weight_scratch[2 * py + px, pl.ds(at, 16), k : k + MIDDLE_CHANNELS] = (
                            columns[px][tx].astype(BF16)
                        )
        return carry

    lax.fori_loop(0, OUTPUT_CHANNELS // 16, combine, 0)
    weight_copy = pltpu.make_async_copy(weight_scratch, weight_out, weight_sem)
    weight_copy.start()
    for copy in copies:
        copy.wait()
    weight_copy.wait()


def decode_kernel(
    dest_ref,
    valid_ref,
    cache_slot_ref,
    latent_ref,
    cache_ref,
    edge_ref,
    feature_ref,
    in_weight_ref,
    in_bias_ref,
    gain_ref,
    time_weight_hbm,
    time_bias_ref,
    out_weight_hbm,
    out_bias_ref,
    out_ref,
    count_ref,
    work_ref,
    patch_ref,
    seq_ref,
    shift_ref,
    low_ref,
    high_ref,
    stage_ref,
    zero_ref,
    time_weight_ref,
    out_weight_ref,
    weight_sem,
    feature_sem,
    zero_sem,
    stage_sem,
):
    group = lax.axis_index("req")
    tile = lax.axis_index("tile")
    tiles = lax.axis_size("tile")

    time_copy = pltpu.make_async_copy(time_weight_hbm, time_weight_ref, weight_sem.at[0])
    out_copy = pltpu.make_async_copy(out_weight_hbm, out_weight_ref, weight_sem.at[1])
    time_copy.start()
    out_copy.start()

    def feature_copies(slot, row):
        place = pl.ds(slot * SEQ, 2)
        return (
            pltpu.make_async_copy(
                feature_ref.at[row],
                seq_ref.at[place, WIDTH : WIDTH + ROWS * WIDTH, :],
                feature_sem.at[0, slot],
            ),
            pltpu.make_async_copy(
                edge_ref.at[0, slot], seq_ref.at[place, 0:WIDTH, :], feature_sem.at[1, slot]
            ),
            pltpu.make_async_copy(
                edge_ref.at[1, slot],
                seq_ref.at[place, WINDOW - WIDTH : WINDOW, :],
                feature_sem.at[2, slot],
            ),
        )

    total = jnp.int32(0)
    last = jnp.int32(0)
    for source in range(4):
        first, second, seen = pick_two(dest_ref, 4 * source, group)
        for k, local in ((0, first), (1, second)):
            slot = 2 * source + k
            r = 4 * source + local
            count = jnp.where(seen > k, valid_ref[r], 0)
            count_ref[slot] = count
            row = cache_slot_ref[r]
            for f in range(FRAMES):
                work_ref[total] = jnp.int32(slot * FRAMES + f)
                keep = f < count
                last = jnp.where(keep, slot * FRAMES + f, last)
                total = total + keep.astype(jnp.int32)

            @pl.when(count > 0)
            def _():
                for copy in feature_copies(slot, row):
                    copy.start()

    for extra in range(GROUP):
        work_ref[total + extra] = last

    zero_ref[...] = jnp.zeros_like(zero_ref)

    def zero_copy(i):
        return pltpu.make_async_copy(
            zero_ref, out_ref.at[i // FRAMES, pl.ds(2 * (i % FRAMES), 2)], zero_sem.at[i]
        )

    @pl.loop(0, 8 * FRAMES)
    def _(i):
        @pl.when((i % FRAMES) >= count_ref[i // FRAMES])
        def _():
            zero_copy(i).start()

    lane = lax.broadcasted_iota(jnp.int32, (LATENT_CHANNELS, 128), 1)
    column = lane % WIDTH

    @pl.loop(0, 8)
    def _(slot):
        count = count_ref[slot]

        @pl.when(count > 0)
        def _():
            turn = lax.rem(group - slot // 2 + 4, 4)
            k = slot % 2
            for pair in range(3):
                blocks = []
                for place in range(3):
                    if pair == 0:
                        block = cache_ref[place, slot].astype(F32)
                    else:
                        block = latent_ref[place, turn, k, pair - 1].astype(F32)
                        frame = 2 * (pair - 1) + lane // 64
                        block = jnp.where(frame < count, block, 0.0)
                    if place == 0:
                        block = jnp.where(tile > 0, block, 0.0)
                    if place == 2:
                        block = jnp.where(tile < tiles - 1, block, 0.0)
                    blocks.append(block)
                up, own, down = blocks

                def turned(value, by):
                    return pltpu.roll(value, by % 128, 1)

                own_half = turned(own, 64)
                windows = (
                    (
                        jnp.where(lane < 64, up, own_half),
                        jnp.where(
                            lane < 32,
                            turned(up, -32),
                            jnp.where(lane < 96, turned(own, 32), turned(down, -32)),
                        ),
                        jnp.where(lane < 64, own, turned(down, 64)),
                    ),
                    (
                        jnp.where(lane < 64, turned(up, 64), own),
                        jnp.where(
                            lane < 32,
                            turned(up, 32),
                            jnp.where(lane < 96, turned(own, -32), turned(down, 32)),
                        ),
                        jnp.where(lane < 64, own_half, down),
                    ),
                )
                for half in range(2):
                    base = (slot * SEQ + 2 * pair + half) * PATCH
                    for b in range(3):
                        window = windows[half][b]
                        shifted = (
                            jnp.where(column == 0, 0.0, turned(window, 1)),
                            window,
                            jnp.where(column == WIDTH - 1, 0.0, turned(window, -1)),
                        )
                        for c in range(3):
                            at = pl.multiple_of(base + (3 * b + c) * 16, 16)
                            patch_ref[pl.ds(at, 16), :] = shifted[c].astype(BF16)

    steps = (total + GROUP - 1) // GROUP

    @pl.loop(0, steps)
    def _(step):
        places = []
        pieces = []
        for u in range(GROUP):
            item = work_ref[step * GROUP + u]
            place = (item // FRAMES) * SEQ + item % FRAMES
            places.append(place)
            at = pl.multiple_of(place * PATCH, 16)
            pieces.append(patch_ref[pl.ds(at, 3 * PATCH), :])
        stacked = jnp.concatenate(pieces, axis=1)
        inner = (
            lax.dot_general(
                stacked,
                in_weight_ref[...],
                (((0,), (0,)), ((), ())),
                preferred_element_type=F32,
            )
            + in_bias_ref[...]
        )
        scale = lax.rsqrt(jnp.mean(inner * inner, axis=-1, keepdims=True) + EPSILON)
        active = jax.nn.silu(inner * scale * gain_ref[...]).astype(BF16)
        for u in range(GROUP):
            seq_ref[places[u] + 2] = active[u * WINDOW : (u + 1) * WINDOW]

    for slot in range(8):

        @pl.when(count_ref[slot] > 0)
        def _():
            for copy in feature_copies(slot, 0):
                copy.wait()

    time_copy.wait()
    out_copy.wait()

    pixel = lax.broadcasted_iota(jnp.int32, (WINDOW, 2 * MIDDLE_CHANNELS), 0)
    inside = ((pixel >= WIDTH) | (tile > 0)) & ((pixel < WINDOW - WIDTH) | (tile < tiles - 1))
    pixel_column = pixel % WIDTH

    def stage_copy(buffer, u, item):
        return pltpu.make_async_copy(
            stage_ref.at[buffer, u],
            out_ref.at[item // FRAMES, pl.ds(2 * (item % FRAMES), 2)],
            stage_sem.at[buffer, u],
        )

    @pl.loop(0, steps)
    def _(step):
        buffer = step % 2
        items = [work_ref[step * GROUP + u] for u in range(GROUP)]
        rows = []
        for u in range(GROUP):
            place = (items[u] // FRAMES) * SEQ + items[u] % FRAMES
            rows.append(jnp.concatenate([seq_ref[place + a] for a in range(3)], axis=1))
        doubled = (
            jnp.dot(
                jnp.concatenate(rows, axis=0), time_weight_ref[...], preferred_element_type=F32
            )
            + time_bias_ref[...]
        )
        for u in range(GROUP):
            own = doubled[u * WINDOW : (u + 1) * WINDOW].astype(BF16).astype(F32)
            own = jnp.where(inside, own, 0.0)
            before = jnp.where(pixel_column == 0, 0.0, pltpu.roll(own, 1, 0))
            after = jnp.where(pixel_column == WIDTH - 1, 0.0, pltpu.roll(own, WINDOW - 1, 0))
            for c, value in enumerate((before, own, after)):
                value = value.astype(BF16)
                for h in range(2):
                    shift_ref[c, 2 * u + h] = value[:, h * MIDDLE_CHANNELS : (h + 1) * MIDDLE_CHANNELS]

        for py in range(2):
            for px in range(2):
                taps = []
                for ty in range(2):
                    for tx in range(2):
                        a = (py + ty) * WIDTH
                        taps.append(
                            shift_ref[px + tx, :, a : a + ROWS * WIDTH, :].reshape(
                                2 * GROUP * ROWS * WIDTH, MIDDLE_CHANNELS
                            )
                        )
                result = (
                    lax.dot_general(
                        jnp.concatenate(taps, axis=1),
                        out_weight_ref[2 * py + px],
                        (((1,), (1,)), ((), ())),
                        preferred_element_type=F32,
                    )
                    + out_bias_ref[...]
                )
                for q in range(2 * GROUP):
                    for y in range(ROWS):
                        at = (q * ROWS + y) * WIDTH
                        spread = pl.ds(px, WIDTH, stride=2)
                        part = result[at : at + WIDTH]
                        low_ref[q, 2 * y + py, spread, :] = part[:, :128]
                        high_ref[q, 2 * y + py, spread, 0 : OUTPUT_CHANNELS - 128] = part[:, 128:]

        @pl.when(step >= 2)
        def _():
            for u in range(GROUP):
                stage_copy(buffer, u, 0).wait()

        for u in range(GROUP):
            stage_ref[buffer, u, :, :, :, 0:128] = low_ref[2 * u : 2 * u + 2].astype(BF16)
            stage_ref[buffer, u, :, :, :, 128:OUTPUT_CHANNELS] = high_ref[
                2 * u : 2 * u + 2, :, :, 0 : OUTPUT_CHANNELS - 128
            ].astype(BF16)
            if u == 0:
                stage_copy(buffer, u, items[u]).start()
            else:

                @pl.when(step * GROUP + u < total)
                def _():
                    stage_copy(buffer, u, items[u]).start()

    for back in range(2, 0, -1):

        @pl.when(steps >= back)
        def _():
            step = steps - back
            for u in range(GROUP):

                @pl.when(step * GROUP + u < total)
                def _():
                    stage_copy(step % 2, u, 0).wait()

    @pl.loop(0, 8 * FRAMES)
    def _(i):
        @pl.when((i % FRAMES) >= count_ref[i // FRAMES])
        def _():
            zero_copy(i).wait()


def per_device(
    latent,
    destination,
    valid_frames,
    cache_slot,
    latent_cache,
    feature_cache,
    in_weight,
    in_bias,
    norm_gain,
    time_weight,
    time_bias,
    out_weight,
    out_bias,
):
    groups = lax.axis_size("req")
    tiles = lax.axis_size("tile")
    target = destination[:, 0]
    smem = pl.BlockSpec(memory_space=pltpu.SMEM)
    vmem = pl.BlockSpec(memory_space=pltpu.VMEM)
    hbm = pl.BlockSpec(memory_space=pl.ANY)
    shape = jax.ShapeDtypeStruct
    dma = pltpu.SemaphoreType.DMA
    slots = 8

    latents, cached, edges, phase_weight = pl.pallas_call(
        functools.partial(exchange_kernel, groups, tiles),
        out_shape=(
            shape((3, 4, CAPACITY, 2, LATENT_CHANNELS, 128), BF16),
            shape((3, slots, LATENT_CHANNELS, 128), BF16),
            shape((2, slots, 2, WIDTH, MIDDLE_CHANNELS), BF16),
            shape((4, OUTPUT_CHANNELS, 4 * MIDDLE_CHANNELS), BF16),
        ),
        in_specs=[smem, smem, vmem, vmem, vmem, vmem],
        out_specs=(hbm, hbm, hbm, hbm),
        scratch_shapes=[
            pltpu.VMEM((4, CAPACITY, 2, LATENT_CHANNELS, 128), BF16),
            pltpu.VMEM((slots, LATENT_CHANNELS, 128), BF16),
            pltpu.VMEM((2, slots, 2, WIDTH, MIDDLE_CHANNELS), BF16),
            pltpu.VMEM((4, OUTPUT_CHANNELS, 4 * MIDDLE_CHANNELS), BF16),
            dma((3, 4)),
            dma((3, 4)),
            dma((3,)),
            dma((3,)),
            dma((2,)),
            dma((2,)),
            dma(()),
        ],
        compiler_params=pltpu.CompilerParams(
            collective_id=0, has_side_effects=True, vmem_limit_bytes=40 * 2**20
        ),
        name="exchange",
    )(
        target,
        cache_slot,
        jnp.transpose(latent, (0, 1, 2, 4, 3)),
        jnp.transpose(latent_cache, (0, 1, 2, 4, 3)),
        feature_cache,
        jnp.transpose(out_weight, (0, 1, 3, 2)),
    )

    return pl.pallas_call(
        decode_kernel,
        out_shape=shape((slots, 2 * FRAMES, 2 * ROWS, 2 * WIDTH, OUTPUT_CHANNELS), BF16),
        in_specs=[smem, smem, smem, vmem, vmem, hbm, hbm, vmem, vmem, vmem, hbm, vmem, hbm, vmem],
        out_specs=hbm,
        scratch_shapes=[
            pltpu.SMEM((slots,), jnp.int32),
            pltpu.SMEM((slots * FRAMES + GROUP,), jnp.int32),
            pltpu.VMEM((slots * SEQ * PATCH, WINDOW), BF16),
            pltpu.VMEM((slots * SEQ, WINDOW, MIDDLE_CHANNELS), BF16),
            pltpu.VMEM((3, 2 * GROUP, WINDOW, MIDDLE_CHANNELS), BF16),
            pltpu.VMEM((2 * GROUP, 2 * ROWS, 2 * WIDTH, 128), F32),
            pltpu.VMEM((2 * GROUP, 2 * ROWS, 2 * WIDTH, 128), F32),
            pltpu.VMEM((2, GROUP, 2, 2 * ROWS, 2 * WIDTH, OUTPUT_CHANNELS), BF16),
            pltpu.VMEM((2, 2 * ROWS, 2 * WIDTH, OUTPUT_CHANNELS), BF16),
            pltpu.VMEM((3 * MIDDLE_CHANNELS, 2 * MIDDLE_CHANNELS), BF16),
            pltpu.VMEM((4, OUTPUT_CHANNELS, 4 * MIDDLE_CHANNELS), BF16),
            dma((2,)),
            dma((3, slots)),
            dma((slots * FRAMES,)),
            dma((2, GROUP)),
        ],
        compiler_params=pltpu.CompilerParams(vmem_limit_bytes=56 * 2**20),
        name="decode",
    )(
        target,
        valid_frames,
        cache_slot,
        latents,
        cached,
        edges,
        feature_cache.reshape(16, 2, ROWS * WIDTH, MIDDLE_CHANNELS),
        in_weight.reshape(27 * LATENT_CHANNELS, MIDDLE_CHANNELS),
        in_bias.reshape(1, -1),
        norm_gain.reshape(1, -1),
        time_weight.reshape(3 * MIDDLE_CHANNELS, 2 * MIDDLE_CHANNELS),
        time_bias.reshape(1, -1),
        phase_weight,
        out_bias.reshape(1, -1),
    )


def solution(mesh):
    placed = (
        P("req", None, "tile", None, None),
        P(),
        P(),
        P(),
        P("req", None, "tile", None, None),
        P("req", None, "tile", None, None),
        P(),
        P(),
        P(),
        P(),
        P(),
        P(),
        P(),
    )
    return jax.shard_map(
        per_device,
        mesh=mesh,
        in_specs=placed,
        out_specs=P("req", None, "tile", None, None),
        check_vma=False,
    )
```

time: 364 us -> 49.7 us (0.14)
  the two profiles are of different devices: /device:TPU:6 before, /device:TPU:8 now
where the time goes in v1:
time: 49.7 us; the launch traced here: 49.3 us
  Pallas kernels  36 us (72%)
  local copies, waits for them, and re-layouts  13.3 us (27%)
    pallas_call x1, Pallas kernels, per_device(): pl.pallas_call(decode_kernel, out_shape=shape((slots, 2 * FRAMES, 2 * ROW...  19.9 us
    pallas_call x1, Pallas kernels, per_device(): pl.pallas_call(functools.partial(exchange_kernel, groups, tiles), out_sha...  16.1 us
    unnamed x20, local copies, waits for them, and re-layouts  9.49 us
    reshape x1, local copies, waits for them, and re-layouts, per_device(): in_bias.reshape(1, -1)  1.28 us
    reshape x1, local copies, waits for them, and re-layouts, per_device(): norm_gain.reshape(1, -1)  1.27 us
    reshape x1, local copies, waits for them, and re-layouts, per_device(): time_bias.reshape(1, -1)  1.26 us

profile of v1, /device:TPU:8, one launch (start us, length us, event | category | flops | bytes accessed | tf_op | source)
XLA Modules:
  0.0 49.3 jit_solution(3063410323058543305)
XLA Ops:
  0.0 1.3 %reshape.23.in_bias_ref = f32[1,384]{1,0:T(1,128)} reshape(f32[384]{0:T(512)} %param.20) | data formatting | bytes 3072 | tf_op jit(solution)/shard_map/reshape | solution.py:569
  1.3 1.3 %reshape.24.gain_ref = f32[1,384]{1,0:T(1,128)} reshape(f32[384]{0:T(512)} %param.21) | data formatting | bytes 3072 | tf_op jit(solution)/shard_map/reshape | solution.py:570
  2.5 1.3 %reshape.26.time_bias_ref = f32[1,768]{1,0:T(1,128)} reshape(f32[768]{0:T(1024)} %param.23) | data formatting | bytes 6144 | tf_op jit(solution)/shard_map/reshape | solution.py:572
  3.8 0.0 copy-start
  3.8 1.4 %copy-done = bf16[16,2,2,32,384]{4,3,2,1,0:T(8,128)(2,1)S(1)} copy-done((bf16[16,2,2,32,384]{4,3,2,1,0:T(8,128)(2,1)S(1)}, bf16[16,2,2,32,384]{4,3,2,1,0:T(8,128)(2,1)}, u32[]{:S(2)}) %copy-start) | copy-done | bytes 1572888
  5.2 0.0 copy-start.2
  5.2 1.3 %copy-done.2 = bf16[3,3,384,192]{2,3,1,0:T(8,128)(2,1)S(1)} copy-done((bf16[3,3,384,192]{2,3,1,0:T(8,128)(2,1)S(1)}, bf16[3,3,384,192]{2,3,1,0:T(8,128)(2,1)}, u32[]{:S(2)}) %copy-start.2) | copy-done | bytes 1327128
  6.5 0.0 copy-start.4
  6.5 0.9 %copy-done.4 = bf16[16,2,2,32,16]{3,4,2,1,0:T(8,128)(2,1)S(1)} copy-done((bf16[16,2,2,32,16]{3,4,2,1,0:T(8,128)(2,1)S(1)}, bf16[16,2,2,32,16]{3,4,2,1,0:T(8,128)(2,1)}, u32[]{:S(2)}) %copy-start.4) | copy-done | bytes 65560
  7.5 0.0 copy-start.6
  7.5 0.9 %copy-done.6 = bf16[4,4,2,32,16]{3,4,2,1,0:T(8,128)(2,1)S(1)} copy-done((bf16[4,4,2,32,16]{3,4,2,1,0:T(8,128)(2,1)S(1)}, bf16[4,4,2,32,16]{3,4,2,1,0:T(8,128)(2,1)}, u32[]{:S(2)}) %copy-start.6) | copy-done | bytes 32792
  8.4 0.0 copy-start.8
  8.4 0.7 %copy-done.8 = s32[16,1]{0,1:T(1,128)S(1)} copy-done((s32[16,1]{0,1:T(1,128)S(1)}, s32[16,1]{0,1:T(1,128)}, u32[]{:S(2)}) %copy-start.8) | copy-done | bytes 88
  9.1 0.0 copy-start.9
  9.1 0.7 %copy-done.9 = s32[16]{0:T(128)S(1)} copy-done((s32[16]{0:T(128)S(1)}, s32[16]{0:T(128)}, u32[]{:S(2)}) %copy-start.9) | copy-done | bytes 88
  9.7 16.1 %exchange.1 = (bf16[3,4,2,2,16,128]{5,4,3,2,1,0:T(8,128)(2,1)S(1)}, bf16[3,8,16,128]{3,2,1,0:T(8,128)(2,1)S(1)}, bf16[2,8,2,32,384]{4,3,2,1,0:T(8,128)(2,1)S(1)}, bf16[4,192,1536]{2,1,0:T(8,128)(2,1)S(1)}) custom-call(s32[16]{0:T(128)S(1)} %bitcast.13, s32[16]{0:T(128)S(1)} %copy-done.9, bf16[4,4,2,16,32]{4,3,2,1,0:T(8,128)(2,1)S(1)} %bitcast.11, ...), custom_call_target="tpu_custom_call" | custom-call | tf_op jit(solution)/shard_map/exchange/pallas_call | solution.py:500
  25.8 0.0 copy-start.1
  25.8 1.4 %copy-done.1 = bf16[4,192,1536]{2,1,0:T(8,128)(2,1)} copy-done((bf16[4,192,1536]{2,1,0:T(8,128)(2,1)}, bf16[4,192,1536]{2,1,0:T(8,128)(2,1)S(1)}, u32[]{:S(2)}) %copy-start.1) | copy-done | bytes 2359320
  27.2 0.0 copy-start.3
  27.2 0.9 %copy-done.3 = bf16[2,8,2,32,384]{4,3,2,1,0:T(8,128)(2,1)} copy-done((bf16[2,8,2,32,384]{4,3,2,1,0:T(8,128)(2,1)}, bf16[2,8,2,32,384]{4,3,2,1,0:T(8,128)(2,1)S(1)}, u32[]{:S(2)}) %copy-start.3) | copy-done | bytes 786456
  28.1 0.0 copy-start.5
  28.1 0.7 %copy-done.5 = bf16[3,4,2,2,16,128]{5,4,3,2,1,0:T(8,128)(2,1)} copy-done((bf16[3,4,2,2,16,128]{5,4,3,2,1,0:T(8,128)(2,1)}, bf16[3,4,2,2,16,128]{5,4,3,2,1,0:T(8,128)(2,1)S(1)}, u32[]{:S(2)}) %copy-start.5) | copy-done | bytes 196632
  28.8 0.0 copy-start.7
  28.8 0.6 %copy-done.7 = bf16[3,8,16,128]{3,2,1,0:T(8,128)(2,1)} copy-done((bf16[3,8,16,128]{3,2,1,0:T(8,128)(2,1)}, bf16[3,8,16,128]{3,2,1,0:T(8,128)(2,1)S(1)}, u32[]{:S(2)}) %copy-start.7) | copy-done | bytes 98328
  29.5 19.9 %decode.1 = bf16[8,8,4,64,192]{4,3,2,1,0:T(8,128)(2,1)} custom-call(s32[16]{0:T(128)} %bitcast.12, s32[16]{0:T(128)} %valid_ref.1, s32[16]{0:T(128)} %cache_slot_ref.3, bf16[3,4,2,2,16,128]{5,4,3,2,1,0:T(8,128)(2,1)} %copy-done.5, bf16[3,8,16,128]{3,2,1,0:T(8,128)(2,1)} %copy-done.7, bf16[2,8,2,32,384]{4,3,2,1,0:T(8,128)(2,1)} %copy-done.3, ...), custom_call_target="tpu_custom_call" | custom-call | tf_op jit(solution)/shard_map/decode/pallas_call | solution.py:536
Async XLA Ops:
  3.8 1.4 %copy-start = (bf16[16,2,2,32,384]{4,3,2,1,0:T(8,128)(2,1)S(1)}, bf16[16,2,2,32,384]{4,3,2,1,0:T(8,128)(2,1)}, u32[]{:S(2)}) copy-start(bf16[16,2,2,32,384]{4,3,2,1,0:T(8,128)(2,1)} %feature_ref.1) | copy-start | bytes 4718596
  5.2 1.3 %copy-start.2 = (bf16[3,3,384,192]{2,3,1,0:T(8,128)(2,1)S(1)}, bf16[3,3,384,192]{2,3,1,0:T(8,128)(2,1)}, u32[]{:S(2)}) copy-start(bf16[3,3,384,192]{2,3,1,0:T(8,128)(2,1)} %param.24) | copy-start | bytes 3981316
  6.5 0.9 %copy-start.4 = (bf16[16,2,2,32,16]{3,4,2,1,0:T(8,128)(2,1)S(1)}, bf16[16,2,2,32,16]{3,4,2,1,0:T(8,128)(2,1)}, u32[]{:S(2)}) copy-start(bf16[16,2,2,32,16]{3,4,2,1,0:T(8,128)(2,1)} %param.17) | copy-start | bytes 196612
  7.5 0.9 %copy-start.6 = (bf16[4,4,2,32,16]{3,4,2,1,0:T(8,128)(2,1)S(1)}, bf16[4,4,2,32,16]{3,4,2,1,0:T(8,128)(2,1)}, u32[]{:S(2)}) copy-start(bf16[4,4,2,32,16]{3,4,2,1,0:T(8,128)(2,1)} %param.13) | copy-start | bytes 98308
  8.4 0.7 %copy-start.8 = (s32[16,1]{0,1:T(1,128)S(1)}, s32[16,1]{0,1:T(1,128)}, u32[]{:S(2)}) copy-start(s32[16,1]{0,1:T(1,128)} %param.14) | copy-start | bytes 196
  9.1 0.7 %copy-start.9 = (s32[16]{0:T(128)S(1)}, s32[16]{0:T(128)}, u32[]{:S(2)}) copy-start(s32[16]{0:T(128)} %cache_slot_ref.3) | copy-start | bytes 196
  25.8 1.4 %copy-start.1 = (bf16[4,192,1536]{2,1,0:T(8,128)(2,1)}, bf16[4,192,1536]{2,1,0:T(8,128)(2,1)S(1)}, u32[]{:S(2)}) copy-start(bf16[4,192,1536]{2,1,0:T(8,128)(2,1)S(1)} %get-tuple-element.12.out_weight_hbm) | copy-start | bytes 7077892
  27.2 0.9 %copy-start.3 = (bf16[2,8,2,32,384]{4,3,2,1,0:T(8,128)(2,1)}, bf16[2,8,2,32,384]{4,3,2,1,0:T(8,128)(2,1)S(1)}, u32[]{:S(2)}) copy-start(bf16[2,8,2,32,384]{4,3,2,1,0:T(8,128)(2,1)S(1)} %get-tuple-element.11.edge_ref) | copy-start | bytes 2359300
  28.1 0.7 %copy-start.5 = (bf16[3,4,2,2,16,128]{5,4,3,2,1,0:T(8,128)(2,1)}, bf16[3,4,2,2,16,128]{5,4,3,2,1,0:T(8,128)(2,1)S(1)}, u32[]{:S(2)}) copy-start(bf16[3,4,2,2,16,128]{5,4,3,2,1,0:T(8,128)(2,1)S(1)} %get-tuple-element.9.latent_ref) | copy-start | bytes 589828
  28.8 0.6 %copy-start.7 = (bf16[3,8,16,128]{3,2,1,0:T(8,128)(2,1)}, bf16[3,8,16,128]{3,2,1,0:T(8,128)(2,1)S(1)}, u32[]{:S(2)}) copy-start(bf16[3,8,16,128]{3,2,1,0:T(8,128)(2,1)S(1)} %get-tuple-element.10.cache_ref) | copy-start | bytes 294916

commit v2 on v1

--- a/solution.py
+++ b/solution.py
@@ -20,6 +20,7 @@
 PATCH = 9 * LATENT_CHANNELS
 SEQ = FRAMES + 2
 GROUP = 2
+VMEM_LIMIT = 63 * 2**20
 
 MESH = pl.DeviceIdType.MESH
 BF16 = jnp.bfloat16
@@ -47,14 +48,18 @@
     tiles,
     dest_ref,
     cache_slot_ref,
+    latent_hbm,
+    latent_cache_hbm,
+    feature_hbm,
+    out_weight_hbm,
+    latent_out,
+    cache_out,
+    feature_out,
+    weight_out,
     latent_ref,
     latent_cache_ref,
     feature_ref,
     out_weight_ref,
-    latent_out,
-    cache_out,
-    feature_out,
-    weight_out,
     latent_send,
     cache_send,
     feature_send,
@@ -66,9 +71,23 @@
     feature_ssem,
     feature_rsem,
     weight_sem,
+    load_sem,
 ):
     group = lax.axis_index("req")
     tile = lax.axis_index("tile")
+    loads = [
+        pltpu.make_async_copy(source, target, load_sem.at[i])
+        for i, (source, target) in enumerate(
+            (
+                (feature_hbm, feature_ref),
+                (latent_cache_hbm, latent_cache_ref),
+                (latent_hbm, latent_ref),
+                (out_weight_hbm, out_weight_ref),
+            )
+        )
+    ]
+    for load in loads:
+        load.start()
 
     def peer(offset, turn):
         return (lax.rem(group + turn, groups), lax.rem(tile + offset + tiles, tiles))
@@ -79,6 +98,8 @@
             if offset or turn:
                 pl.semaphore_signal(barrier, inc=1, device_id=peer(offset, turn), device_id_type=MESH)
 
+    for load in loads[:3]:
+        load.wait()
     for source in range(4):
         first, second, _ = pick_two(dest_ref, 4 * source, group)
         for k, local in ((0, first), (1, second)):
@@ -146,6 +167,7 @@
             )
     for copy in copies:
         copy.start()
+    loads[3].wait()
 
     def combine(i, carry):
         at = pl.multiple_of(i * 16, 16)
@@ -356,10 +378,10 @@
                 (((0,), (0,)), ((), ())),
                 preferred_element_type=F32,
             )
-            + in_bias_ref[...]
+            + in_bias_ref[...][None, :]
         )
         scale = lax.rsqrt(jnp.mean(inner * inner, axis=-1, keepdims=True) + EPSILON)
-        active = jax.nn.silu(inner * scale * gain_ref[...]).astype(BF16)
+        active = jax.nn.silu(inner * scale * gain_ref[...][None, :]).astype(BF16)
         for u in range(GROUP):
             seq_ref[places[u] + 2] = active[u * WINDOW : (u + 1) * WINDOW]
 
@@ -396,7 +418,7 @@
             jnp.dot(
                 jnp.concatenate(rows, axis=0), time_weight_ref[...], preferred_element_type=F32
             )
-            + time_bias_ref[...]
+            + time_bias_ref[...][None, :]
         )
         for u in range(GROUP):
             own = doubled[u * WINDOW : (u + 1) * WINDOW].astype(BF16).astype(F32)
@@ -426,7 +448,7 @@
                         (((1,), (1,)), ((), ())),
                         preferred_element_type=F32,
                     )
-                    + out_bias_ref[...]
+                    + out_bias_ref[...][None, :]
                 )
                 for q in range(2 * GROUP):
                     for y in range(ROWS):
@@ -505,9 +527,13 @@
             shape((2, slots, 2, WIDTH, MIDDLE_CHANNELS), BF16),
             shape((4, OUTPUT_CHANNELS, 4 * MIDDLE_CHANNELS), BF16),
         ),
-        in_specs=[smem, smem, vmem, vmem, vmem, vmem],
+        in_specs=[smem, smem, hbm, hbm, hbm, hbm],
         out_specs=(hbm, hbm, hbm, hbm),
         scratch_shapes=[
+            pltpu.VMEM((4, FRAMES, ROWS, LATENT_CHANNELS, WIDTH), BF16),
+            pltpu.VMEM((16, 2, ROWS, LATENT_CHANNELS, WIDTH), BF16),
+            pltpu.VMEM((16, 2, ROWS, WIDTH, MIDDLE_CHANNELS), BF16),
+            pltpu.VMEM((3, 3, OUTPUT_CHANNELS, MIDDLE_CHANNELS), BF16),
             pltpu.VMEM((4, CAPACITY, 2, LATENT_CHANNELS, 128), BF16),
             pltpu.VMEM((slots, LATENT_CHANNELS, 128), BF16),
             pltpu.VMEM((2, slots, 2, WIDTH, MIDDLE_CHANNELS), BF16),
@@ -519,9 +545,10 @@
             dma((2,)),
             dma((2,)),
             dma(()),
+            dma((4,)),
         ],
         compiler_params=pltpu.CompilerParams(
-            collective_id=0, has_side_effects=True, vmem_limit_bytes=40 * 2**20
+            collective_id=0, has_side_effects=True, vmem_limit_bytes=VMEM_LIMIT
         ),
         name="exchange",
     )(
@@ -555,7 +582,7 @@
             dma((slots * FRAMES,)),
             dma((2, GROUP)),
         ],
-        compiler_params=pltpu.CompilerParams(vmem_limit_bytes=56 * 2**20),
+        compiler_params=pltpu.CompilerParams(vmem_limit_bytes=VMEM_LIMIT),
         name="decode",
     )(
         target,
@@ -566,12 +593,12 @@
         edges,
         feature_cache.reshape(16, 2, ROWS * WIDTH, MIDDLE_CHANNELS),
         in_weight.reshape(27 * LATENT_CHANNELS, MIDDLE_CHANNELS),
-        in_bias.reshape(1, -1),
-        norm_gain.reshape(1, -1),
+        in_bias,
+        norm_gain,
         time_weight.reshape(3 * MIDDLE_CHANNELS, 2 * MIDDLE_CHANNELS),
-        time_bias.reshape(1, -1),
+        time_bias,
         phase_weight,
-        out_bias.reshape(1, -1),
+        out_bias,
     )
 
 

time: 49.7 us -> 35.4 us (0.71)
  the two profiles are of different devices: /device:TPU:8 before, /device:TPU:0 now
where the time goes in v2:
time: 35.4 us; the launch traced here: 35.3 us
  Pallas kernels  35.2 us (99%)
    pallas_call x1, Pallas kernels, per_device(): pl.pallas_call(decode_kernel, out_shape=shape((slots, 2 * FRAMES, 2 * ROW...  17.8 us
    pallas_call x1, Pallas kernels, per_device(): pl.pallas_call(functools.partial(exchange_kernel, groups, tiles), out_sha...  17.5 us

profile of v2, /device:TPU:0, one launch (start us, length us, event | category | flops | bytes accessed | tf_op | source)
XLA Modules:
  0.0 35.3 jit_solution(15739495537325632172)
XLA Ops:
  0.0 17.5 %exchange.1 = (bf16[3,4,2,2,16,128]{5,4,3,2,1,0:T(8,128)(2,1)}, bf16[3,8,16,128]{3,2,1,0:T(8,128)(2,1)}, bf16[2,8,2,32,384]{4,3,2,1,0:T(8,128)(2,1)}, bf16[4,192,1536]{2,1,0:T(8,128)(2,1)}) custom-call(s32[16]{0:T(128)} %bitcast.13, s32[16]{0:T(128)} %cache_slot_ref.3, bf16[4,4,2,16,32]{4,3,2,1,0:T(8,128)(2,1)} %bitcast.12, ...), custom_call_target="tpu_custom_call" | custom-call | tf_op jit(solution)/shard_map/exchange/pallas_call | solution.py:522
  17.5 17.8 %decode.1 = bf16[8,8,4,64,192]{4,3,2,1,0:T(8,128)(2,1)} custom-call(s32[16]{0:T(128)} %bitcast.14, s32[16]{0:T(128)} %valid_ref.1, s32[16]{0:T(128)} %cache_slot_ref.3, bf16[3,4,2,2,16,128]{5,4,3,2,1,0:T(8,128)(2,1)} %get-tuple-element.9.latent_ref, bf16[3,8,16,128]{3,2,1,0:T(8,128)(2,1)} %get-tuple-element.10.cache_ref, ...), custom_call_target="tpu_custom_call" | custom-call | tf_op jit(solution)/shard_map/decode/pallas_call | solution.py:563

commit v3 on v2

v3 whole, which is shorter than its diff:
```python
import functools

import jax
import jax.numpy as jnp
from jax import lax
from jax.experimental import pallas as pl
from jax.experimental.pallas import tpu as pltpu
from jax.sharding import PartitionSpec as P

LATENT_CHANNELS = 16
MIDDLE_CHANNELS = 384
OUTPUT_CHANNELS = 192
FRAMES = 4
CAPACITY = 2
EPSILON = 1e-06

ROWS = 2
WIDTH = 32
WINDOW = (ROWS + 2) * WIDTH
PATCH = 9 * LATENT_CHANNELS
SEQ = FRAMES + 2
GROUP = 4
VMEM_LIMIT = 28 * 2**20

MESH = pl.DeviceIdType.MESH
BF16 = jnp.bfloat16
F32 = jnp.float32


def pick_two(dest_ref, start, target):
    seen = jnp.int32(0)
    first = jnp.int32(0)
    second = jnp.int32(0)
    for j in range(4):
        hit = dest_ref[start + j] == target
        first = jnp.where(hit & (seen == 0), j, first)
        second = jnp.where(hit & (seen == 1), j, second)
        seen = seen + hit.astype(jnp.int32)
    return first, second, seen


def lane_join(pieces):
    return jnp.concatenate([p.astype(F32) for p in pieces], axis=-1).astype(BF16)


def exchange_kernel(
    groups,
    tiles,
    dest_hbm,
    valid_hbm,
    cache_slot_hbm,
    latent_hbm,
    latent_cache_hbm,
    feature_hbm,
    out_weight_hbm,
    cached_ref,
    patch_ref,
    phase_ref,
    dest_ref,
    valid_ref,
    cache_slot_ref,
    latent_ref,
    latent_cache_ref,
    feature_ref,
    out_weight_ref,
    latent_send,
    cache_send,
    feature_send,
    latent_recv,
    cache_recv,
    count_ref,
    latent_ssem,
    latent_rsem,
    cache_ssem,
    cache_rsem,
    feature_ssem,
    feature_rsem,
    load_sem,
):
    group = lax.axis_index("req")
    tile = lax.axis_index("tile")
    loads = [
        pltpu.make_async_copy(source, target, load_sem.at[i])
        for i, (source, target) in enumerate(
            (
                (dest_hbm, dest_ref),
                (cache_slot_hbm, cache_slot_ref),
                (valid_hbm, valid_ref),
                (latent_hbm, latent_ref),
                (latent_cache_hbm, latent_cache_ref),
                (feature_hbm, feature_ref),
                (out_weight_hbm, out_weight_ref),
            )
        )
    ]
    for load in loads:
        load.start()

    def peer(offset, turn):
        return (lax.rem(group + turn, groups), lax.rem(tile + offset + tiles, tiles))

    present = {-1: tile > 0, 0: None, 1: tile < tiles - 1}

    def where_present(offset, act):
        def run():
            act()

        if offset == 0:
            run()
        else:
            pl.when(present[offset])(run)

    barrier = pltpu.get_barrier_semaphore()
    for offset in (-1, 0, 1):

        def greet():
            for turn in range(4):
                if offset or turn:
                    pl.semaphore_signal(
                        barrier, inc=1, device_id=peer(offset, turn), device_id_type=MESH
                    )

        where_present(offset, greet)

    for load in loads[:3]:
        load.wait()

    cache_rows = []
    for source in range(4):
        first, second, seen = pick_two(dest_ref, 4 * source, group)
        for k, local in ((0, first), (1, second)):
            r = 4 * source + local
            cache_rows.append(cache_slot_ref[r])
            count_ref[2 * source + k] = jnp.where(seen > k, valid_ref[r], 0)
    picks = [
        pick_two(dest_ref, 4 * group, lax.rem(group + turn, groups))[:2] for turn in range(4)
    ]

    loads[3].wait()
    for turn in range(4):
        for k in range(CAPACITY):
            for pair in range(2):
                block = lane_join(
                    [latent_ref[picks[turn][k], 2 * pair + f, y] for f in range(2) for y in range(2)]
                )
                latent_send[turn, k, pair] = block
                if turn == 0:
                    latent_recv[1, 0, k, pair] = block
    loads[4].wait()
    for slot in range(8):
        block = lane_join(
            [latent_cache_ref[cache_rows[slot], f, y] for f in range(2) for y in range(2)]
        )
        cache_send[slot] = block
        cache_recv[1, slot] = block

    sides = (tile > 0).astype(jnp.int32) + (tile < tiles - 1).astype(jnp.int32)
    pl.semaphore_wait(barrier, 3 + 4 * sides)
    sends = {}
    arrivals = {}
    for offset in (1, -1, 0):
        place = 1 - offset
        sends[offset] = []
        if offset:
            sends[offset].append(
                pltpu.make_async_remote_copy(
                    src_ref=cache_send,
                    dst_ref=cache_recv.at[place],
                    send_sem=cache_ssem.at[place],
                    recv_sem=cache_rsem.at[place],
                    device_id=peer(offset, 0),
                    device_id_type=MESH,
                )
            )
        for turn in range(4):
            if offset or turn:
                sends[offset].append(
                    pltpu.make_async_remote_copy(
                        src_ref=latent_send.at[turn],
                        dst_ref=latent_recv.at[place, turn],
                        send_sem=latent_ssem.at[place, turn],
                        recv_sem=latent_rsem.at[place, turn],
                        device_id=peer(offset, turn),
                        device_id_type=MESH,
                    )
                )
        arrivals[-offset] = sends[offset]
    for offset in (1, -1, 0):
        where_present(offset, lambda: [copy.start() for copy in sends[offset]])

    loads[5].wait()
    for slot in range(8):
        for f in range(2):
            for edge in range(2):
                feature_send[edge, slot, f] = feature_ref[cache_rows[slot], f, edge]
    edges = {
        offset: pltpu.make_async_remote_copy(
            src_ref=feature_send.at[edge],
            dst_ref=cached_ref.at[:, :, at : at + WIDTH, :],
            send_sem=feature_ssem.at[edge],
            recv_sem=feature_rsem.at[edge],
            device_id=peer(offset, 0),
            device_id_type=MESH,
        )
        for edge, offset, at in ((1, 1, 0), (0, -1, WINDOW - WIDTH))
    }
    for offset in (1, -1):
        where_present(offset, lambda: edges[offset].start())
    for slot in range(8):
        for f in range(2):
            for y in range(ROWS):
                at = (1 + y) * WIDTH
                cached_ref[slot, f, at : at + WIDTH, :] = feature_send[y, slot, f]
    loads[6].wait()

    def combine(i, carry):
        at = pl.multiple_of(i * 16, 16)
        taps = [
            [out_weight_ref[b, c, pl.ds(at, 16), :].astype(F32) for c in range(3)] for b in range(3)
        ]
        rows = (
            (taps[0], [u + v for u, v in zip(taps[1], taps[2])]),
            ([u + v for u, v in zip(taps[0], taps[1])], taps[2]),
        )
        for py in range(2):
            for ty in range(2):
                line = rows[py][ty]
                columns = ((line[0], line[1] + line[2]), (line[0] + line[1], line[2]))
                for px in range(2):
                    for tx in range(2):
                        k = (2 * ty + tx) * MIDDLE_CHANNELS
                        phase_ref[2 * py + px, pl.ds(at, 16), k : k + MIDDLE_CHANNELS] = columns[px][
                            tx
                        ].astype(BF16)
        return carry

    lax.fori_loop(0, OUTPUT_CHANNELS // 16, combine, 0)
    for offset in (1, -1, 0):
        where_present(offset, lambda: [copy.wait_recv() for copy in arrivals[offset]])

    lane = lax.broadcasted_iota(jnp.int32, (LATENT_CHANNELS, 128), 1)
    column = lane % WIDTH

    def turned(value, by):
        return pltpu.roll(value, by % 128, 1)

    def gather_patches(slot, carry):
        count = count_ref[slot]
        turn = lax.rem(group - slot // 2 + 4, 4)
        k = slot % 2
        for pair in range(3):
            blocks = []
            for place in range(3):
                if pair == 0:
                    block = cache_recv[place, slot].astype(F32)
                else:
                    block = latent_recv[place, turn, k, pair - 1].astype(F32)
                    frame = 2 * (pair - 1) + lane // 64
                    block = jnp.where(frame < count, block, 0.0)
                if place == 0:
                    block = jnp.where(tile > 0, block, 0.0)
                if place == 2:
                    block = jnp.where(tile < tiles - 1, block, 0.0)
                blocks.append(block)
            up, own, down = blocks
            own_half = turned(own, 64)
            windows = (
                (
                    jnp.where(lane < 64, up, own_half),
                    jnp.where(
                        lane < 32,
                        turned(up, -32),
                        jnp.where(lane < 96, turned(own, 32), turned(down, -32)),
                    ),
                    jnp.where(lane < 64, own, turned(down, 64)),
                ),
                (
                    jnp.where(lane < 64, turned(up, 64), own),
                    jnp.where(
                        lane < 32,
                        turned(up, 32),
                        jnp.where(lane < 96, turned(own, -32), turned(down, 32)),
                    ),
                    jnp.where(lane < 64, own_half, down),
                ),
            )
            for half in range(2):
                base = (slot * SEQ + 2 * pair + half) * PATCH
                for b in range(3):
                    window = windows[half][b]
                    shifted = (
                        jnp.where(column == 0, 0.0, turned(window, 1)),
                        window,
                        jnp.where(column == WIDTH - 1, 0.0, turned(window, -1)),
                    )
                    for c in range(3):
                        at = pl.multiple_of(base + (3 * b + c) * 16, 16)
                        patch_ref[pl.ds(at, 16), :] = shifted[c].astype(BF16)
        return carry

    lax.fori_loop(0, 8, gather_patches, 0)
    for offset in (1, -1, 0):
        where_present(offset, lambda: [copy.wait_send() for copy in sends[offset]])
    for offset in (1, -1):
        where_present(offset, lambda: edges[offset].wait_send())
        where_present(-offset, lambda: edges[offset].wait_recv())

    for edge, gone in ((0, tile == 0), (WINDOW - WIDTH, tile == tiles - 1)):

        @pl.when(gone)
        def _():
            cached_ref[:, :, edge : edge + WIDTH, :] = jnp.zeros(
                (8, 2, WIDTH, MIDDLE_CHANNELS), BF16
            )


def decode_kernel(
    dest_ref,
    valid_ref,
    cached_ref,
    patch_ref,
    in_weight_ref,
    in_bias_ref,
    gain_ref,
    time_weight_ref,
    time_bias_ref,
    out_weight_ref,
    out_bias_ref,
    out_ref,
    count_ref,
    work_ref,
    seq_ref,
    shift_ref,
    low_ref,
    high_ref,
    stage_ref,
    zero_ref,
    zero_sem,
    stage_sem,
):
    group = lax.axis_index("req")
    tile = lax.axis_index("tile")
    tiles = lax.axis_size("tile")

    total = jnp.int32(0)
    last = jnp.int32(0)
    for source in range(4):
        first, second, seen = pick_two(dest_ref, 4 * source, group)
        for k, local in ((0, first), (1, second)):
            slot = 2 * source + k
            count = jnp.where(seen > k, valid_ref[4 * source + local], 0)
            count_ref[slot] = count
            for f in range(FRAMES):
                work_ref[total] = jnp.int32(slot * FRAMES + f)
                keep = f < count
                last = jnp.where(keep, slot * FRAMES + f, last)
                total = total + keep.astype(jnp.int32)
    for extra in range(2 * GROUP):
        work_ref[total + extra] = last
    steps = (total + GROUP - 1) // GROUP

    zero_ref[...] = jnp.zeros_like(zero_ref)

    def zero_copy(i):
        return pltpu.make_async_copy(
            zero_ref, out_ref.at[i // FRAMES, pl.ds(2 * (i % FRAMES), 2)], zero_sem.at[i]
        )

    @pl.loop(0, 8 * FRAMES)
    def _(i):
        @pl.when((i % FRAMES) >= count_ref[i // FRAMES])
        def _():
            zero_copy(i).start()

    for slot in range(8):

        @pl.when(count_ref[slot] > 0)
        def _():
            seq_ref[slot, 0:2] = cached_ref[slot]

    half_gain = 0.5 * gain_ref[...][None, :]
    in_bias = in_bias_ref[...][None, :]

    def in_conv(step):
        for part in range(GROUP // 2):
            places = []
            pieces = []
            for u in range(2):
                item = work_ref[step * GROUP + 2 * part + u]
                slot, f = item // FRAMES, item % FRAMES
                places.append((slot, f))
                at = pl.multiple_of((slot * SEQ + f) * PATCH, 16)
                pieces.append(patch_ref[pl.ds(at, 3 * PATCH), :])
            inner = (
                lax.dot_general(
                    jnp.concatenate(pieces, axis=1),
                    in_weight_ref[...],
                    (((0,), (0,)), ((), ())),
                    preferred_element_type=F32,
                )
                + in_bias
            )
            scale = lax.rsqrt(jnp.mean(inner * inner, axis=-1, keepdims=True) + EPSILON)
            half = inner * scale * half_gain
            active = (half + half * jnp.tanh(half)).astype(BF16)
            for u, (slot, f) in enumerate(places):
                seq_ref[slot, f + 2] = active[u * WINDOW : (u + 1) * WINDOW]

    pixel = lax.broadcasted_iota(jnp.int32, (WINDOW, 2 * MIDDLE_CHANNELS), 0)
    inside = ((pixel >= WIDTH) | (tile > 0)) & ((pixel < WINDOW - WIDTH) | (tile < tiles - 1))
    pixel_column = pixel % WIDTH

    def stage_copy(buffer, u, item):
        return pltpu.make_async_copy(
            stage_ref.at[buffer, u],
            out_ref.at[item // FRAMES, pl.ds(2 * (item % FRAMES), 2)],
            stage_sem.at[buffer, u],
        )

    @pl.when(steps > 0)
    def _():
        in_conv(0)

    @pl.loop(0, steps)
    def _(step):
        buffer = step % 2
        items = [work_ref[step * GROUP + u] for u in range(GROUP)]
        rows = []
        for u in range(GROUP):
            slot, f = items[u] // FRAMES, items[u] % FRAMES
            rows.append(jnp.concatenate([seq_ref[slot, f + a] for a in range(3)], axis=1))
        doubled = (
            jnp.dot(
                jnp.concatenate(rows, axis=0), time_weight_ref[...], preferred_element_type=F32
            )
            + time_bias_ref[...][None, :]
        )
        in_conv(step + 1)
        for u in range(GROUP):
            own = doubled[u * WINDOW : (u + 1) * WINDOW].astype(BF16).astype(F32)
            own = jnp.where(inside, own, 0.0)
            before = jnp.where(pixel_column == 0, 0.0, pltpu.roll(own, 1, 0))
            after = jnp.where(pixel_column == WIDTH - 1, 0.0, pltpu.roll(own, WINDOW - 1, 0))
            for c, value in enumerate((before, own, after)):
                value = value.astype(BF16)
                for h in range(2):
                    shift_ref[c, 2 * u + h] = value[:, h * MIDDLE_CHANNELS : (h + 1) * MIDDLE_CHANNELS]

        for py in range(2):
            for px in range(2):
                taps = []
                for ty in range(2):
                    for tx in range(2):
                        a = (py + ty) * WIDTH
                        taps.append(
                            shift_ref[px + tx, :, a : a + ROWS * WIDTH, :].reshape(
                                2 * GROUP * ROWS * WIDTH, MIDDLE_CHANNELS
                            )
                        )
                result = (
                    lax.dot_general(
                        jnp.concatenate(taps, axis=1),
                        out_weight_ref[2 * py + px],
                        (((1,), (1,)), ((), ())),
                        preferred_element_type=F32,
                    )
                    + out_bias_ref[...][None, :]
                )
                for q in range(2 * GROUP):
                    for y in range(ROWS):
                        at = (q * ROWS + y) * WIDTH
                        spread = pl.ds(px, WIDTH, stride=2)
                        part = result[at : at + WIDTH]
                        low_ref[q, 2 * y + py, spread, :] = part[:, :128]
                        high_ref[q, 2 * y + py, spread, 0 : OUTPUT_CHANNELS - 128] = part[:, 128:]

        @pl.when(step >= 2)
        def _():
            for u in range(GROUP):
                stage_copy(buffer, u, 0).wait()

        for u in range(GROUP):
            stage_ref[buffer, u, :, :, :, 0:128] = low_ref[2 * u : 2 * u + 2].astype(BF16)
            stage_ref[buffer, u, :, :, :, 128:OUTPUT_CHANNELS] = high_ref[
                2 * u : 2 * u + 2, :, :, 0 : OUTPUT_CHANNELS - 128
            ].astype(BF16)
            if u == 0:
                stage_copy(buffer, u, items[u]).start()
            else:

                @pl.when(step * GROUP + u < total)
                def _():
                    stage_copy(buffer, u, items[u]).start()

    for back in range(2, 0, -1):

        @pl.when(steps >= back)
        def _():
            step = steps - back
            for u in range(GROUP):

                @pl.when(step * GROUP + u < total)
                def _():
                    stage_copy(step % 2, u, 0).wait()

    @pl.loop(0, 8 * FRAMES)
    def _(i):
        @pl.when((i % FRAMES) >= count_ref[i // FRAMES])
        def _():
            zero_copy(i).wait()


def per_device(
    latent,
    destination,
    valid_frames,
    cache_slot,
    latent_cache,
    feature_cache,
    in_weight,
    in_bias,
    norm_gain,
    time_weight,
    time_bias,
    out_weight,
    out_bias,
):
    groups = lax.axis_size("req")
    tiles = lax.axis_size("tile")
    target = destination[:, 0]
    smem = pl.BlockSpec(memory_space=pltpu.SMEM)
    vmem = pl.BlockSpec(memory_space=pltpu.VMEM)
    hbm = pl.BlockSpec(memory_space=pltpu.HBM)
    shape = jax.ShapeDtypeStruct
    dma = pltpu.SemaphoreType.DMA
    slots = 8

    in_hbm = functools.partial(pltpu.with_memory_space_constraint, memory_space=pltpu.HBM)

    cached, patches, phase_weight = pl.pallas_call(
        functools.partial(exchange_kernel, groups, tiles),
        out_shape=(
            pltpu.VMEM((slots, 2, WINDOW, MIDDLE_CHANNELS), BF16),
            pltpu.VMEM((slots * SEQ * PATCH, WINDOW), BF16),
            pltpu.VMEM((4, OUTPUT_CHANNELS, 4 * MIDDLE_CHANNELS), BF16),
        ),
        in_specs=[hbm] * 7,
        out_specs=(vmem, vmem, vmem),
        scratch_shapes=[
            pltpu.SMEM((16,), jnp.int32),
            pltpu.SMEM((16,), jnp.int32),
            pltpu.SMEM((16,), jnp.int32),
            pltpu.VMEM((4, FRAMES, ROWS, LATENT_CHANNELS, WIDTH), BF16),
            pltpu.VMEM((16, 2, ROWS, LATENT_CHANNELS, WIDTH), BF16),
            pltpu.VMEM((16, 2, ROWS, WIDTH, MIDDLE_CHANNELS), BF16),
            pltpu.VMEM((3, 3, OUTPUT_CHANNELS, MIDDLE_CHANNELS), BF16),
            pltpu.VMEM((4, CAPACITY, 2, LATENT_CHANNELS, 128), BF16),
            pltpu.VMEM((slots, LATENT_CHANNELS, 128), BF16),
            pltpu.VMEM((2, slots, 2, WIDTH, MIDDLE_CHANNELS), BF16),
            pltpu.VMEM((3, 4, CAPACITY, 2, LATENT_CHANNELS, 128), BF16),
            pltpu.VMEM((3, slots, LATENT_CHANNELS, 128), BF16),
            pltpu.SMEM((slots,), jnp.int32),
            dma((3, 4)),
            dma((3, 4)),
            dma((3,)),
            dma((3,)),
            dma((2,)),
            dma((2,)),
            dma((7,)),
        ],
        compiler_params=pltpu.CompilerParams(
            collective_id=0, has_side_effects=True, vmem_limit_bytes=VMEM_LIMIT
        ),
        name="exchange",
    )(
        in_hbm(target),
        in_hbm(valid_frames),
        in_hbm(cache_slot),
        in_hbm(jnp.transpose(latent, (0, 1, 2, 4, 3))),
        in_hbm(jnp.transpose(latent_cache, (0, 1, 2, 4, 3))),
        in_hbm(feature_cache),
        in_hbm(jnp.transpose(out_weight, (0, 1, 3, 2))),
    )

    return pl.pallas_call(
        decode_kernel,
        out_shape=shape((slots, 2 * FRAMES, 2 * ROWS, 2 * WIDTH, OUTPUT_CHANNELS), BF16),
        in_specs=[smem, smem] + [vmem] * 9,
        out_specs=hbm,
        scratch_shapes=[
            pltpu.SMEM((slots,), jnp.int32),
            pltpu.SMEM((slots * FRAMES + 2 * GROUP,), jnp.int32),
            pltpu.VMEM((slots, SEQ, WINDOW, MIDDLE_CHANNELS), BF16),
            pltpu.VMEM((3, 2 * GROUP, WINDOW, MIDDLE_CHANNELS), BF16),
            pltpu.VMEM((2 * GROUP, 2 * ROWS, 2 * WIDTH, 128), F32),
            pltpu.VMEM((2 * GROUP, 2 * ROWS, 2 * WIDTH, 128), F32),
            pltpu.VMEM((2, GROUP, 2, 2 * ROWS, 2 * WIDTH, OUTPUT_CHANNELS), BF16),
            pltpu.VMEM((2, 2 * ROWS, 2 * WIDTH, OUTPUT_CHANNELS), BF16),
            dma((slots * FRAMES,)),
            dma((2, GROUP)),
        ],
        compiler_params=pltpu.CompilerParams(vmem_limit_bytes=VMEM_LIMIT),
        name="decode",
    )(
        target,
        valid_frames,
        cached,
        patches,
        in_weight.reshape(27 * LATENT_CHANNELS, MIDDLE_CHANNELS),
        in_bias,
        norm_gain,
        time_weight.reshape(3 * MIDDLE_CHANNELS, 2 * MIDDLE_CHANNELS),
        time_bias,
        phase_weight,
        out_bias,
    )


def solution(mesh):
    placed = (
        P("req", None, "tile", None, None),
        P(),
        P(),
        P(),
        P("req", None, "tile", None, None),
        P("req", None, "tile", None, None),
        P(),
        P(),
        P(),
        P(),
        P(),
        P(),
        P(),
    )
    return jax.shard_map(
        per_device,
        mesh=mesh,
        in_specs=placed,
        out_specs=P("req", None, "tile", None, None),
        check_vma=False,
    )
```

time: 35.4 us -> 32.7 us (0.924)
  the two profiles are of different devices: /device:TPU:0 before, /device:TPU:30 now
where the time goes in v3:
time: 32.7 us; the launch traced here: 32.6 us
  Pallas kernels  32.5 us (99%)
    pallas_call x1, Pallas kernels, per_device(): pl.pallas_call(decode_kernel, out_shape=shape((slots, 2 * FRAMES, 2 * ROW...  19.8 us
    pallas_call x1, Pallas kernels, per_device(): pl.pallas_call(functools.partial(exchange_kernel, groups, tiles), out_sha...  12.7 us

profile of v3, /device:TPU:30, one launch (start us, length us, event | category | flops | bytes accessed | tf_op | source)
XLA Modules:
  0.0 32.6 jit_solution(13932561385311909261)
XLA Ops:
  0.0 0.0 copy-start.6
  0.0 0.0 copy-start.7
  0.0 0.0 copy-start.2
  0.0 0.0 copy-start
  0.0 0.0 copy-start.4
  0.0 0.0 copy-start.3
  0.0 0.0 copy-start.1
  0.0 0.0 copy-start.5
  0.1 12.7 %exchange.1 = (bf16[8,2,128,384]{3,2,1,0:T(8,128)(2,1)S(1)}, bf16[6912,128]{1,0:T(8,128)(2,1)S(1)}, bf16[4,192,1536]{2,1,0:T(8,128)(2,1)S(1)}) custom-call(s32[16]{0:T(128)} %bitcast.8, s32[16]{0:T(128)} %valid_ref.1, s32[16]{0:T(128)} %cache_slot_hbm.1, bf16[4,4,2,16,32]{4,3,2,1,0:T(8,128)(2,1)} %bitcast.12, bf16[16,2,2,16,32]{4,3,2,1,0:T(8,128)(2,1)} %bitcast.11, ...), custom_call_target="tpu_custom_call" | custom-call | tf_op jit(solution)/shard_map/exchange/pallas_call | solution.py:540
  12.7 0.0 copy-done.6
  12.8 0.0 copy-done.7
  12.8 0.0 copy-done.2
  12.8 0.0 copy-done
  12.8 0.0 copy-done.4
  12.8 0.0 copy-done.3
  12.8 0.0 copy-done.1
  12.8 0.0 copy-done.5
  12.8 19.8 %decode.1 = bf16[8,8,4,64,192]{4,3,2,1,0:T(8,128)(2,1)} custom-call(s32[16]{0:T(128)S(1)} %bitcast.9, s32[16]{0:T(128)S(1)} %copy-done.6, bf16[8,2,128,384]{3,2,1,0:T(8,128)(2,1)S(1)} %get-tuple-element.8.cached_ref, bf16[6912,128]{1,0:T(8,128)(2,1)S(1)} %get-tuple-element.9.patch_ref, bf16[432,384]{1,0:T(8,128)(2,1)S(1)} %bitcast.7, f32[384]{0:T(512)S(1)} %copy-done.3, ...), custom_call_target="tpu_custom_call" | custom-call | tf_op jit(solution)/shard_map/decode/pallas_call | solution.py:585
Async XLA Ops:
  0.0 12.8 %copy-start.6 = (s32[16]{0:T(128)S(1)}, s32[16]{0:T(128)}, u32[]{:S(2)}) copy-start(s32[16]{0:T(128)} %valid_ref.1) | copy-start | bytes 196
  0.0 12.8 %copy-start.7 = (f32[192]{0:T(256)S(1)}, f32[192]{0:T(256)}, u32[]{:S(2)}) copy-start(f32[192]{0:T(256)} %out_bias_ref.1) | copy-start | bytes 2308
  0.0 12.8 %copy-start.2 = (f32[768]{0:T(1024)S(1)}, f32[768]{0:T(1024)}, u32[]{:S(2)}) copy-start(f32[768]{0:T(1024)} %time_bias_ref.1) | copy-start | bytes 9220
  0.0 12.8 %copy-start = (bf16[3,384,768]{2,1,0:T(8,128)(2,1)S(1)}, bf16[3,384,768]{2,1,0:T(8,128)(2,1)}, u32[]{:S(2)}) copy-start(bf16[3,384,768]{2,1,0:T(8,128)(2,1)} %param.22) | copy-start | bytes 5308420
  0.0 12.8 %copy-start.4 = (f32[384]{0:T(512)S(1)}, f32[384]{0:T(512)}, u32[]{:S(2)}) copy-start(f32[384]{0:T(512)} %gain_ref.1) | copy-start | bytes 4612
  0.0 12.8 %copy-start.3 = (f32[384]{0:T(512)S(1)}, f32[384]{0:T(512)}, u32[]{:S(2)}) copy-start(f32[384]{0:T(512)} %in_bias_ref.1) | copy-start | bytes 4612
  0.0 12.8 %copy-start.1 = (bf16[3,3,3,16,384]{4,3,2,1,0:T(8,128)(2,1)S(1)}, bf16[3,3,3,16,384]{4,3,2,1,0:T(8,128)(2,1)}, u32[]{:S(2)}) copy-start(bf16[3,3,3,16,384]{4,3,2,1,0:T(8,128)(2,1)} %param.19) | copy-start | bytes 995332
  0.0 12.8 %copy-start.5 = (s32[16,1]{0,1:T(1,128)S(1)}, s32[16,1]{0,1:T(1,128)}, u32[]{:S(2)}) copy-start(s32[16,1]{0,1:T(1,128)} %param.14) | copy-start | bytes 196

commit v4 on v3

--- a/solution.py
+++ b/solution.py
@@ -63,16 +63,15 @@
     latent_cache_ref,
     feature_ref,
     out_weight_ref,
-    latent_send,
-    cache_send,
+    packed_ref,
     feature_send,
-    latent_recv,
-    cache_recv,
+    near_ref,
+    far_ref,
     count_ref,
-    latent_ssem,
-    latent_rsem,
-    cache_ssem,
-    cache_rsem,
+    near_ssem,
+    near_rsem,
+    far_ssem,
+    far_rsem,
     feature_ssem,
     feature_rsem,
     load_sem,
@@ -93,8 +92,6 @@
             )
         )
     ]
-    for load in loads:
-        load.start()
 
     def peer(offset, turn):
         return (lax.rem(group + turn, groups), lax.rem(tile + offset + tiles, tiles))
@@ -111,16 +108,17 @@
             pl.when(present[offset])(run)
 
     barrier = pltpu.get_barrier_semaphore()
-    for offset in (-1, 0, 1):
-
-        def greet():
-            for turn in range(4):
-                if offset or turn:
-                    pl.semaphore_signal(
-                        barrier, inc=1, device_id=peer(offset, turn), device_id_type=MESH
-                    )
-
-        where_present(offset, greet)
+    for offset in (1, -1):
+        where_present(
+            offset,
+            lambda: pl.semaphore_signal(
+                barrier, inc=1, device_id=peer(offset, 0), device_id_type=MESH
+            ),
+        )
+    for turn in range(1, 4):
+        pl.semaphore_signal(barrier, inc=1, device_id=peer(0, turn), device_id_type=MESH)
+    for load in loads:
+        load.start()
 
     for load in loads[:3]:
         load.wait()
@@ -143,50 +141,32 @@
                 block = lane_join(
                     [latent_ref[picks[turn][k], 2 * pair + f, y] for f in range(2) for y in range(2)]
                 )
-                latent_send[turn, k, pair] = block
-                if turn == 0:
-                    latent_recv[1, 0, k, pair] = block
+                at = 4 * turn + 2 * k + pair
+                packed_ref[at] = block
+                near_ref[1, at] = block
     loads[4].wait()
     for slot in range(8):
         block = lane_join(
             [latent_cache_ref[cache_rows[slot], f, y] for f in range(2) for y in range(2)]
         )
-        cache_send[slot] = block
-        cache_recv[1, slot] = block
+        packed_ref[16 + slot] = block
+        near_ref[1, 16 + slot] = block
 
     sides = (tile > 0).astype(jnp.int32) + (tile < tiles - 1).astype(jnp.int32)
-    pl.semaphore_wait(barrier, 3 + 4 * sides)
-    sends = {}
-    arrivals = {}
-    for offset in (1, -1, 0):
-        place = 1 - offset
-        sends[offset] = []
-        if offset:
-            sends[offset].append(
-                pltpu.make_async_remote_copy(
-                    src_ref=cache_send,
-                    dst_ref=cache_recv.at[place],
-                    send_sem=cache_ssem.at[place],
-                    recv_sem=cache_rsem.at[place],
-                    device_id=peer(offset, 0),
-                    device_id_type=MESH,
-                )
-            )
-        for turn in range(4):
-            if offset or turn:
-                sends[offset].append(
-                    pltpu.make_async_remote_copy(
-                        src_ref=latent_send.at[turn],
-                        dst_ref=latent_recv.at[place, turn],
-                        send_sem=latent_ssem.at[place, turn],
-                        recv_sem=latent_rsem.at[place, turn],
-                        device_id=peer(offset, turn),
-                        device_id_type=MESH,
-                    )
-                )
-        arrivals[-offset] = sends[offset]
-    for offset in (1, -1, 0):
-        where_present(offset, lambda: [copy.start() for copy in sends[offset]])
+    pl.semaphore_wait(barrier, 3 + sides)
+    near = {
+        offset: pltpu.make_async_remote_copy(
+            src_ref=packed_ref,
+            dst_ref=near_ref.at[1 - offset],
+            send_sem=near_ssem.at[1 - offset],
+            recv_sem=near_rsem.at[1 - offset],
+            device_id=peer(offset, 0),
+            device_id_type=MESH,
+        )
+        for offset in (1, -1)
+    }
+    for offset in (1, -1):
+        where_present(offset, lambda: near[offset].start())
 
     loads[5].wait()
     for slot in range(8):
@@ -211,6 +191,30 @@
             for y in range(ROWS):
                 at = (1 + y) * WIDTH
                 cached_ref[slot, f, at : at + WIDTH, :] = feature_send[y, slot, f]
+    for place, gone in ((0, tile == 0), (2, tile == tiles - 1)):
+
+        @pl.when(gone)
+        def _():
+            near_ref[place] = jnp.zeros((24, LATENT_CHANNELS, 128), BF16)
+
+    for offset in (1, -1):
+        where_present(-offset, lambda: near[offset].wait_recv())
+    far = []
+    for turn in (2, 1, 3):
+        part = pl.ds(4 * turn, 4)
+        far.append(
+            pltpu.make_async_remote_copy(
+                src_ref=near_ref.at[:, part],
+                dst_ref=far_ref.at[:, part],
+                send_sem=far_ssem.at[turn],
+                recv_sem=far_rsem.at[turn],
+                device_id=peer(0, turn),
+                device_id_type=MESH,
+            )
+        )
+    for copy in far:
+        copy.start()
+    far_ref[:, 0:4] = near_ref[:, 0:4]
     loads[6].wait()
 
     def combine(i, carry):
@@ -224,19 +228,17 @@
         )
         for py in range(2):
             for ty in range(2):
-                line = rows[py][ty]
-                columns = ((line[0], line[1] + line[2]), (line[0] + line[1], line[2]))
-                for px in range(2):
-                    for tx in range(2):
-                        k = (2 * ty + tx) * MIDDLE_CHANNELS
-                        phase_ref[2 * py + px, pl.ds(at, 16), k : k + MIDDLE_CHANNELS] = columns[px][
-                            tx
-                        ].astype(BF16)
+                left, middle, right = rows[py][ty]
+                k = ty * MIDDLE_CHANNELS
+                for part, value in enumerate((left, left + middle + right, right)):
+                    phase_ref[3 * py + part, pl.ds(at, 16), k : k + MIDDLE_CHANNELS] = value.astype(
+                        BF16
+                    )
         return carry
 
     lax.fori_loop(0, OUTPUT_CHANNELS // 16, combine, 0)
-    for offset in (1, -1, 0):
-        where_present(offset, lambda: [copy.wait_recv() for copy in arrivals[offset]])
+    for copy in far:
+        copy.wait_recv()
 
     lane = lax.broadcasted_iota(jnp.int32, (LATENT_CHANNELS, 128), 1)
     column = lane % WIDTH
@@ -252,9 +254,9 @@
             blocks = []
             for place in range(3):
                 if pair == 0:
-                    block = cache_recv[place, slot].astype(F32)
+                    block = near_ref[place, 16 + slot].astype(F32)
                 else:
-                    block = latent_recv[place, turn, k, pair - 1].astype(F32)
+                    block = far_ref[place, 4 * turn + 2 * k + pair - 1].astype(F32)
                     frame = 2 * (pair - 1) + lane // 64
                     block = jnp.where(frame < count, block, 0.0)
                 if place == 0:
@@ -298,10 +300,11 @@
                         patch_ref[pl.ds(at, 16), :] = shifted[c].astype(BF16)
         return carry
 
-    lax.fori_loop(0, 8, gather_patches, 0)
-    for offset in (1, -1, 0):
-        where_present(offset, lambda: [copy.wait_send() for copy in sends[offset]])
+    lax.fori_loop(0, 8, gather_patches, 0, unroll=2)
+    for copy in far:
+        copy.wait_send()
     for offset in (1, -1):
+        where_present(offset, lambda: near[offset].wait_send())
         where_present(offset, lambda: edges[offset].wait_send())
         where_present(-offset, lambda: edges[offset].wait_recv())
 
@@ -361,16 +364,25 @@
 
     zero_ref[...] = jnp.zeros_like(zero_ref)
 
-    def zero_copy(i):
-        return pltpu.make_async_copy(
-            zero_ref, out_ref.at[i // FRAMES, pl.ds(2 * (i % FRAMES), 2)], zero_sem.at[i]
-        )
-
-    @pl.loop(0, 8 * FRAMES)
-    def _(i):
-        @pl.when((i % FRAMES) >= count_ref[i // FRAMES])
-        def _():
-            zero_copy(i).start()
+    def each_zero(act):
+        @pl.loop(0, 8)
+        def _(slot):
+            count = count_ref[slot]
+            missing = FRAMES - count
+            for size in (1, 2, 4):
+                at = 2 * jnp.where(size == 1, count, FRAMES - size)
+
+                @pl.when((missing & size) > 0)
+                def _():
+                    act(
+                        pltpu.make_async_copy(
+                            zero_ref.at[pl.ds(0, 2 * size)],
+                            out_ref.at[slot, pl.ds(at, 2 * size)],
+                            zero_sem.at[slot, size // 2],
+                        )
+                    )
+
+    each_zero(lambda copy: copy.start())
 
     for slot in range(8):
 
@@ -406,9 +418,9 @@
             for u, (slot, f) in enumerate(places):
                 seq_ref[slot, f + 2] = active[u * WINDOW : (u + 1) * WINDOW]
 
-    pixel = lax.broadcasted_iota(jnp.int32, (WINDOW, 2 * MIDDLE_CHANNELS), 0)
-    inside = ((pixel >= WIDTH) | (tile > 0)) & ((pixel < WINDOW - WIDTH) | (tile < tiles - 1))
-    pixel_column = pixel % WIDTH
+    pixel_column = lax.broadcasted_iota(jnp.int32, (WINDOW, 2 * MIDDLE_CHANNELS), 0) % WIDTH
+    first_column = pixel_column == 0
+    last_column = pixel_column == WIDTH - 1
 
     def stage_copy(buffer, u, item):
         return pltpu.make_async_copy(
@@ -435,37 +447,46 @@
             )
             + time_bias_ref[...][None, :]
         )
-        in_conv(step + 1)
         for u in range(GROUP):
-            own = doubled[u * WINDOW : (u + 1) * WINDOW].astype(BF16).astype(F32)
-            own = jnp.where(inside, own, 0.0)
-            before = jnp.where(pixel_column == 0, 0.0, pltpu.roll(own, 1, 0))
-            after = jnp.where(pixel_column == WIDTH - 1, 0.0, pltpu.roll(own, WINDOW - 1, 0))
-            for c, value in enumerate((before, own, after)):
-                value = value.astype(BF16)
+            own = doubled[u * WINDOW : (u + 1) * WINDOW]
+            own = jnp.concatenate(
+                [
+                    jnp.where(tile > 0, own[:WIDTH], 0.0),
+                    own[WIDTH : WINDOW - WIDTH],
+                    jnp.where(tile < tiles - 1, own[WINDOW - WIDTH :], 0.0),
+                ],
+                axis=0,
+            )
+            middle = own.astype(BF16)
+            before = jnp.where(first_column, 0.0, pltpu.roll(own, 1, 0).astype(BF16))
+            after = jnp.where(last_column, 0.0, pltpu.roll(own, WINDOW - 1, 0).astype(BF16))
+            for c, value in enumerate((before - middle, middle, after - middle)):
                 for h in range(2):
                     shift_ref[c, 2 * u + h] = value[:, h * MIDDLE_CHANNELS : (h + 1) * MIDDLE_CHANNELS]
 
+        in_conv(step + 1)
         for py in range(2):
-            for px in range(2):
+            products = []
+            for part in range(3):
                 taps = []
                 for ty in range(2):
-                    for tx in range(2):
-                        a = (py + ty) * WIDTH
-                        taps.append(
-                            shift_ref[px + tx, :, a : a + ROWS * WIDTH, :].reshape(
-                                2 * GROUP * ROWS * WIDTH, MIDDLE_CHANNELS
-                            )
+                    a = (py + ty) * WIDTH
+                    taps.append(
+                        shift_ref[part, :, a : a + ROWS * WIDTH, :].reshape(
+                            2 * GROUP * ROWS * WIDTH, MIDDLE_CHANNELS
                         )
-                result = (
+                    )
+                products.append(
                     lax.dot_general(
                         jnp.concatenate(taps, axis=1),
-                        out_weight_ref[2 * py + px],
+                        out_weight_ref[3 * py + part],
                         (((1,), (1,)), ((), ())),
                         preferred_element_type=F32,
                     )
-                    + out_bias_ref[...][None, :]
                 )
+            shared = products[1] + out_bias_ref[...][None, :]
+            for px in range(2):
+                result = shared + products[2 * px]
                 for q in range(2 * GROUP):
                     for y in range(ROWS):
                         at = (q * ROWS + y) * WIDTH
@@ -503,11 +524,7 @@
                 def _():
                     stage_copy(step % 2, u, 0).wait()
 
-    @pl.loop(0, 8 * FRAMES)
-    def _(i):
-        @pl.when((i % FRAMES) >= count_ref[i // FRAMES])
-        def _():
-            zero_copy(i).wait()
+    each_zero(lambda copy: copy.wait())
 
 
 def per_device(
@@ -542,7 +559,7 @@
         out_shape=(
             pltpu.VMEM((slots, 2, WINDOW, MIDDLE_CHANNELS), BF16),
             pltpu.VMEM((slots * SEQ * PATCH, WINDOW), BF16),
-            pltpu.VMEM((4, OUTPUT_CHANNELS, 4 * MIDDLE_CHANNELS), BF16),
+            pltpu.VMEM((6, OUTPUT_CHANNELS, 2 * MIDDLE_CHANNELS), BF16),
         ),
         in_specs=[hbm] * 7,
         out_specs=(vmem, vmem, vmem),
@@ -554,16 +571,15 @@
             pltpu.VMEM((16, 2, ROWS, LATENT_CHANNELS, WIDTH), BF16),
             pltpu.VMEM((16, 2, ROWS, WIDTH, MIDDLE_CHANNELS), BF16),
             pltpu.VMEM((3, 3, OUTPUT_CHANNELS, MIDDLE_CHANNELS), BF16),
-            pltpu.VMEM((4, CAPACITY, 2, LATENT_CHANNELS, 128), BF16),
-            pltpu.VMEM((slots, LATENT_CHANNELS, 128), BF16),
+            pltpu.VMEM((24, LATENT_CHANNELS, 128), BF16),
             pltpu.VMEM((2, slots, 2, WIDTH, MIDDLE_CHANNELS), BF16),
-            pltpu.VMEM((3, 4, CAPACITY, 2, LATENT_CHANNELS, 128), BF16),
-            pltpu.VMEM((3, slots, LATENT_CHANNELS, 128), BF16),
+            pltpu.VMEM((3, 24, LATENT_CHANNELS, 128), BF16),
+            pltpu.VMEM((3, 16, LATENT_CHANNELS, 128), BF16),
             pltpu.SMEM((slots,), jnp.int32),
-            dma((3, 4)),
-            dma((3, 4)),
             dma((3,)),
             dma((3,)),
+            dma((4,)),
+            dma((4,)),
             dma((2,)),
             dma((2,)),
             dma((7,)),
@@ -595,8 +611,8 @@
             pltpu.VMEM((2 * GROUP, 2 * ROWS, 2 * WIDTH, 128), F32),
             pltpu.VMEM((2 * GROUP, 2 * ROWS, 2 * WIDTH, 128), F32),
             pltpu.VMEM((2, GROUP, 2, 2 * ROWS, 2 * WIDTH, OUTPUT_CHANNELS), BF16),
-            pltpu.VMEM((2, 2 * ROWS, 2 * WIDTH, OUTPUT_CHANNELS), BF16),
-            dma((slots * FRAMES,)),
+            pltpu.VMEM((2 * FRAMES, 2 * ROWS, 2 * WIDTH, OUTPUT_CHANNELS), BF16),
+            dma((slots, 3)),
             dma((2, GROUP)),
         ],
         compiler_params=pltpu.CompilerParams(vmem_limit_bytes=VMEM_LIMIT),

time: 32.7 us -> 30 us (0.917)
  the two profiles are of different devices: /device:TPU:30 before, /device:TPU:6 now
where the time goes in v4:
time: 30 us; the launch traced here: 29.9 us
  Pallas kernels  29.8 us (99%)
    pallas_call x1, Pallas kernels, per_device(): pl.pallas_call(decode_kernel, out_shape=shape((slots, 2 * FRAMES, 2 * ROW...  15 us
    pallas_call x1, Pallas kernels, per_device(): pl.pallas_call(functools.partial(exchange_kernel, groups, tiles), out_sha...  14.8 us

profile of v4, /device:TPU:6, one launch (start us, length us, event | category | flops | bytes accessed | tf_op | source)
XLA Modules:
  0.0 29.9 jit_solution(17158645188908107896)
XLA Ops:
  0.0 0.0 copy-start.6
  0.0 0.0 copy-start.7
  0.0 0.0 copy-start.2
  0.0 0.0 copy-start
  0.0 0.0 copy-start.4
  0.0 0.0 copy-start.3
  0.0 0.0 copy-start.1
  0.0 0.0 copy-start.5
  0.1 14.8 %exchange.1 = (bf16[8,2,128,384]{3,2,1,0:T(8,128)(2,1)S(1)}, bf16[6912,128]{1,0:T(8,128)(2,1)S(1)}, bf16[6,192,768]{2,1,0:T(8,128)(2,1)S(1)}) custom-call(s32[16]{0:T(128)} %bitcast.8, s32[16]{0:T(128)} %valid_ref.1, s32[16]{0:T(128)} %cache_slot_hbm.1, bf16[4,4,2,16,32]{4,3,2,1,0:T(8,128)(2,1)} %bitcast.12, bf16[16,2,2,16,32]{4,3,2,1,0:T(8,128)(2,1)} %bitcast.11, ...), custom_call_target="tpu_custom_call" | custom-call | tf_op jit(solution)/shard_map/exchange/pallas_call | solution.py:557
  14.8 0.0 copy-done.6
  14.8 0.0 copy-done.7
  14.9 0.0 copy-done.2
  14.9 0.0 copy-done
  14.9 0.0 copy-done.4
  14.9 0.0 copy-done.3
  14.9 0.0 copy-done.1
  14.9 0.0 copy-done.5
  14.9 15.0 %decode.1 = bf16[8,8,4,64,192]{4,3,2,1,0:T(8,128)(2,1)} custom-call(s32[16]{0:T(128)S(1)} %bitcast.9, s32[16]{0:T(128)S(1)} %copy-done.6, bf16[8,2,128,384]{3,2,1,0:T(8,128)(2,1)S(1)} %get-tuple-element.8.cached_ref, bf16[6912,128]{1,0:T(8,128)(2,1)S(1)} %get-tuple-element.9.patch_ref, bf16[432,384]{1,0:T(8,128)(2,1)S(1)} %bitcast.7, f32[384]{0:T(512)S(1)} %copy-done.3, ...), custom_call_target="tpu_custom_call" | custom-call | tf_op jit(solution)/shard_map/decode/pallas_call | solution.py:601
Async XLA Ops:
  0.0 14.8 %copy-start.6 = (s32[16]{0:T(128)S(1)}, s32[16]{0:T(128)}, u32[]{:S(2)}) copy-start(s32[16]{0:T(128)} %valid_ref.1) | copy-start | bytes 196
  0.0 14.8 %copy-start.7 = (f32[192]{0:T(256)S(1)}, f32[192]{0:T(256)}, u32[]{:S(2)}) copy-start(f32[192]{0:T(256)} %out_bias_ref.1) | copy-start | bytes 2308
  0.0 14.9 %copy-start.2 = (f32[768]{0:T(1024)S(1)}, f32[768]{0:T(1024)}, u32[]{:S(2)}) copy-start(f32[768]{0:T(1024)} %time_bias_ref.1) | copy-start | bytes 9220
  0.0 14.9 %copy-start = (bf16[3,384,768]{2,1,0:T(8,128)(2,1)S(1)}, bf16[3,384,768]{2,1,0:T(8,128)(2,1)}, u32[]{:S(2)}) copy-start(bf16[3,384,768]{2,1,0:T(8,128)(2,1)} %param.22) | copy-start | bytes 5308420
  0.0 14.9 %copy-start.4 = (f32[384]{0:T(512)S(1)}, f32[384]{0:T(512)}, u32[]{:S(2)}) copy-start(f32[384]{0:T(512)} %gain_ref.1) | copy-start | bytes 4612
  0.0 14.9 %copy-start.3 = (f32[384]{0:T(512)S(1)}, f32[384]{0:T(512)}, u32[]{:S(2)}) copy-start(f32[384]{0:T(512)} %in_bias_ref.1) | copy-start | bytes 4612
  0.0 14.9 %copy-start.1 = (bf16[3,3,3,16,384]{4,3,2,1,0:T(8,128)(2,1)S(1)}, bf16[3,3,3,16,384]{4,3,2,1,0:T(8,128)(2,1)}, u32[]{:S(2)}) copy-start(bf16[3,3,3,16,384]{4,3,2,1,0:T(8,128)(2,1)} %param.19) | copy-start | bytes 995332
  0.0 14.9 %copy-start.5 = (s32[16,1]{0,1:T(1,128)S(1)}, s32[16,1]{0,1:T(1,128)}, u32[]{:S(2)}) copy-start(s32[16,1]{0,1:T(1,128)} %param.14) | copy-start | bytes 196

commit v5 on v4

--- a/solution.py
+++ b/solution.py
@@ -360,7 +360,8 @@
                 total = total + keep.astype(jnp.int32)
     for extra in range(2 * GROUP):
         work_ref[total + extra] = last
-    steps = (total + GROUP - 1) // GROUP
+    steps = (total + 1) // GROUP
+    has_tail = total > steps * GROUP
 
     zero_ref[...] = jnp.zeros_like(zero_ref)
 
@@ -429,16 +430,15 @@
             stage_sem.at[buffer, u],
         )
 
-    @pl.when(steps > 0)
+    @pl.when(total > 0)
     def _():
         in_conv(0)
 
-    @pl.loop(0, steps)
-    def _(step):
+    def decode_items(step, size):
         buffer = step % 2
-        items = [work_ref[step * GROUP + u] for u in range(GROUP)]
+        items = [work_ref[step * GROUP + u] for u in range(size)]
         rows = []
-        for u in range(GROUP):
+        for u in range(size):
             slot, f = items[u] // FRAMES, items[u] % FRAMES
             rows.append(jnp.concatenate([seq_ref[slot, f + a] for a in range(3)], axis=1))
         doubled = (
@@ -447,7 +447,7 @@
             )
             + time_bias_ref[...][None, :]
         )
-        for u in range(GROUP):
+        for u in range(size):
             own = doubled[u * WINDOW : (u + 1) * WINDOW]
             own = jnp.concatenate(
                 [
@@ -464,7 +464,8 @@
                 for h in range(2):
                     shift_ref[c, 2 * u + h] = value[:, h * MIDDLE_CHANNELS : (h + 1) * MIDDLE_CHANNELS]
 
-        in_conv(step + 1)
+        if size == GROUP:
+            in_conv(step + 1)
         for py in range(2):
             products = []
             for part in range(3):
@@ -472,8 +473,8 @@
                 for ty in range(2):
                     a = (py + ty) * WIDTH
                     taps.append(
-                        shift_ref[part, :, a : a + ROWS * WIDTH, :].reshape(
-                            2 * GROUP * ROWS * WIDTH, MIDDLE_CHANNELS
+                        shift_ref[part, 0 : 2 * size, a : a + ROWS * WIDTH, :].reshape(
+                            2 * size * ROWS * WIDTH, MIDDLE_CHANNELS
                         )
                     )
                 products.append(
@@ -487,7 +488,7 @@
             shared = products[1] + out_bias_ref[...][None, :]
             for px in range(2):
                 result = shared + products[2 * px]
-                for q in range(2 * GROUP):
+                for q in range(2 * size):
                     for y in range(ROWS):
                         at = (q * ROWS + y) * WIDTH
                         spread = pl.ds(px, WIDTH, stride=2)
@@ -500,7 +501,7 @@
             for u in range(GROUP):
                 stage_copy(buffer, u, 0).wait()
 
-        for u in range(GROUP):
+        for u in range(size):
             stage_ref[buffer, u, :, :, :, 0:128] = low_ref[2 * u : 2 * u + 2].astype(BF16)
             stage_ref[buffer, u, :, :, :, 128:OUTPUT_CHANNELS] = high_ref[
                 2 * u : 2 * u + 2, :, :, 0 : OUTPUT_CHANNELS - 128
@@ -513,11 +514,20 @@
                 def _():
                     stage_copy(buffer, u, items[u]).start()
 
+    @pl.loop(0, steps)
+    def _(step):
+        decode_items(step, GROUP)
+
+    @pl.when(has_tail)
+    def _():
+        decode_items(steps, GROUP // 2)
+
+    ends = steps + has_tail.astype(jnp.int32)
     for back in range(2, 0, -1):
 
-        @pl.when(steps >= back)
+        @pl.when(ends >= back)
         def _():
-            step = steps - back
+            step = ends - back
             for u in range(GROUP):
 
                 @pl.when(step * GROUP + u < total)

time: 30 us -> 27.9 us (0.930)
  the two profiles are of different devices: /device:TPU:6 before, /device:TPU:14 now
where the time goes in v5:
time: 27.9 us; the launch traced here: 27.8 us
  Pallas kernels  27.7 us (99%)
    pallas_call x1, Pallas kernels, per_device(): pl.pallas_call(functools.partial(exchange_kernel, groups, tiles), out_sha...  13.8 us
    pallas_call x1, Pallas kernels, per_device(): pl.pallas_call(decode_kernel, out_shape=shape((slots, 2 * FRAMES, 2 * ROW...  13.8 us

profile of v5, /device:TPU:14, one launch (start us, length us, event | category | flops | bytes accessed | tf_op | source)
XLA Modules:
  0.0 27.8 jit_solution(1872928005405279069)
XLA Ops:
  0.0 0.0 copy-start.6
  0.0 0.0 copy-start.7
  0.0 0.0 copy-start.2
  0.0 0.0 copy-start
  0.0 0.0 copy-start.4
  0.0 0.0 copy-start.3
  0.0 0.0 copy-start.1
  0.0 0.0 copy-start.5
  0.1 13.8 %exchange.1 = (bf16[8,2,128,384]{3,2,1,0:T(8,128)(2,1)S(1)}, bf16[6912,128]{1,0:T(8,128)(2,1)S(1)}, bf16[6,192,768]{2,1,0:T(8,128)(2,1)S(1)}) custom-call(s32[16]{0:T(128)} %bitcast.8, s32[16]{0:T(128)} %valid_ref.1, s32[16]{0:T(128)} %cache_slot_hbm.1, bf16[4,4,2,16,32]{4,3,2,1,0:T(8,128)(2,1)} %bitcast.12, bf16[16,2,2,16,32]{4,3,2,1,0:T(8,128)(2,1)} %bitcast.11, ...), custom_call_target="tpu_custom_call" | custom-call | tf_op jit(solution)/shard_map/exchange/pallas_call | solution.py:567
  13.9 0.0 copy-done.6
  13.9 0.0 copy-done.7
  13.9 0.0 copy-done.2
  13.9 0.0 copy-done
  14.0 0.0 copy-done.4
  14.0 0.0 copy-done.3
  14.0 0.0 copy-done.1
  14.0 0.0 copy-done.5
  14.0 13.8 %decode.1 = bf16[8,8,4,64,192]{4,3,2,1,0:T(8,128)(2,1)} custom-call(s32[16]{0:T(128)S(1)} %bitcast.9, s32[16]{0:T(128)S(1)} %copy-done.6, bf16[8,2,128,384]{3,2,1,0:T(8,128)(2,1)S(1)} %get-tuple-element.8.cached_ref, bf16[6912,128]{1,0:T(8,128)(2,1)S(1)} %get-tuple-element.9.patch_ref, bf16[432,384]{1,0:T(8,128)(2,1)S(1)} %bitcast.7, f32[384]{0:T(512)S(1)} %copy-done.3, ...), custom_call_target="tpu_custom_call" | custom-call | tf_op jit(solution)/shard_map/decode/pallas_call | solution.py:611
Async XLA Ops:
  0.0 13.9 %copy-start.6 = (s32[16]{0:T(128)S(1)}, s32[16]{0:T(128)}, u32[]{:S(2)}) copy-start(s32[16]{0:T(128)} %valid_ref.1) | copy-start | bytes 196
  0.0 13.9 %copy-start.7 = (f32[192]{0:T(256)S(1)}, f32[192]{0:T(256)}, u32[]{:S(2)}) copy-start(f32[192]{0:T(256)} %out_bias_ref.1) | copy-start | bytes 2308
  0.0 13.9 %copy-start.2 = (f32[768]{0:T(1024)S(1)}, f32[768]{0:T(1024)}, u32[]{:S(2)}) copy-start(f32[768]{0:T(1024)} %time_bias_ref.1) | copy-start | bytes 9220
  0.0 13.9 %copy-start = (bf16[3,384,768]{2,1,0:T(8,128)(2,1)S(1)}, bf16[3,384,768]{2,1,0:T(8,128)(2,1)}, u32[]{:S(2)}) copy-start(bf16[3,384,768]{2,1,0:T(8,128)(2,1)} %param.22) | copy-start | bytes 5308420
  0.0 13.9 %copy-start.4 = (f32[384]{0:T(512)S(1)}, f32[384]{0:T(512)}, u32[]{:S(2)}) copy-start(f32[384]{0:T(512)} %gain_ref.1) | copy-start | bytes 4612
  0.0 13.9 %copy-start.3 = (f32[384]{0:T(512)S(1)}, f32[384]{0:T(512)}, u32[]{:S(2)}) copy-start(f32[384]{0:T(512)} %in_bias_ref.1) | copy-start | bytes 4612
  0.0 13.9 %copy-start.1 = (bf16[3,3,3,16,384]{4,3,2,1,0:T(8,128)(2,1)S(1)}, bf16[3,3,3,16,384]{4,3,2,1,0:T(8,128)(2,1)}, u32[]{:S(2)}) copy-start(bf16[3,3,3,16,384]{4,3,2,1,0:T(8,128)(2,1)} %param.19) | copy-start | bytes 995332
  0.0 13.9 %copy-start.5 = (s32[16,1]{0,1:T(1,128)S(1)}, s32[16,1]{0,1:T(1,128)}, u32[]{:S(2)}) copy-start(s32[16,1]{0,1:T(1,128)} %param.14) | copy-start | bytes 196
